TPU v7x, 256 devices: a whole 4x4x8 slice. The times are simulated.
256 devices in a mesh: atoms: 64 (over y, z, core), pair: 4 (over x).
Axes of the slice: x: 4, y: 4, z: 8, core: 2. Of those that a mesh axis runs over, the one named last changes fastest.
Arguments:
- trunk_single: bfloat16 [6144, 384], P('atoms'), may hold values from -6 to 6
- atom_feature: bfloat16 [49152, 128], P('atoms'), may hold values from -6 to 6
- pair_band: bfloat16 [6144, 256, 128], P('atoms'), may hold values from -6 to 6
- atom_token: int32 [49152], replicated, may hold values from 0 to 6143, as said below
- token_counts: int32 [6144], P('atoms'), may hold values from 1 to 24, as said below
- key_offsets: int32 [1536], P('atoms'), may hold values from -96 to 0
- single_weight: bfloat16 [384, 128], replicated, may hold values from -0.3125 to 0.3125
- attn_weight: bfloat16 [128, 4, 128], P(None, 'pair'), may hold values from -0.5 to 0.5
- bias_weight: float32 [128, 4], P(None, 'pair'), may hold values from -12 to 12
- out_weight: bfloat16 [128, 128], P('pair'), may hold values from -2 to 2
- token_weight: bfloat16 [128, 384], replicated, may hold values from -0.5 to 0.5
Outputs:
- atom_single: bfloat16 [49152, 128], P('atoms')
- token_single: bfloat16 [6144, 384], P('atoms')
Inputs may be any that keep to these rules, and one draw needn't show every extreme that they name: Token i has token_counts[i] atoms. For every g, tokens g * 4 * 96 to (g + 1) * 4 * 96 - 1 have 4 * 768 atoms together. `atom_token`: never falls from one atom to the next; token i is named exactly token_counts[i] times, so atoms g * 4 * 768 to (g + 1) * 4 * 768 - 1 belong to tokens g * 4 * 96 to (g + 1) * 4 * 96 - 1.
All inputs are finite; a program needn't handle non-finite values.
Results may differ from a plain program's by a relative error of at most 0.02.
Values may be sent and summed in bfloat16 or wider, within the bound.
A program may use at most 128 MiB of HBM per device.

v0:
```python
import math

import jax
import jax.numpy as jnp
from jax import lax
from jax.sharding import PartitionSpec as P

GROUP = 4


def from_behind(value, axis, steps):
    count = lax.axis_size(axis)
    leading, last = (max(0, -steps), min(count, count - steps))
    return lax.ppermute(value, axis, [(source, source + steps) for source in range(leading, last)])


def with_halo(block, sides, width):
    for axis, dim in sides:
        count = lax.axis_size(axis)
        forward = [(i, i + 1) for i in range(count - 1)]
        backward = [(target, source) for source, target in forward]
        low = lax.ppermute(
            lax.slice_in_dim(block, block.shape[dim] - width, None, axis=dim), axis, forward
        )
        high = lax.ppermute(lax.slice_in_dim(block, 0, width, axis=dim), axis, backward)
        block = jnp.concatenate([low, block, high], axis=dim)
    return block


def layer_norm(values):
    average = jnp.mean(values, axis=-1, keepdims=True)
    centred = values - average
    spread = jnp.mean(centred * centred, axis=-1, keepdims=True)
    return centred * lax.rsqrt(spread + 1e-05)


def select_rows(carried, shard_rows, first_row, my_tokens):
    row_count = shard_rows.shape[0]
    relative = my_tokens - first_row
    picker = relative[:, None] == jnp.arange(row_count, dtype=jnp.int32)[None, :]
    if shard_rows.dtype == jnp.bfloat16:
        chosen = jnp.dot(
            picker.astype(jnp.bfloat16), shard_rows, preferred_element_type=jnp.float32
        ).astype(jnp.bfloat16)
    else:
        chosen = jnp.dot(picker.astype(jnp.float32), shard_rows, precision=lax.Precision.HIGHEST)
    return carried + chosen


def shards(
    trunk_single,
    atom_feature,
    pair_band,
    atom_token,
    token_counts,
    key_offsets,
    single_weight,
    attn_weight,
    bias_weight,
    out_weight,
    token_weight,
):
    tok_dev = trunk_single.shape[0]
    atom_dev = atom_feature.shape[0]
    win_dev = key_offsets.shape[0]
    total_atoms = atom_token.shape[0]
    heads_here = bias_weight.shape[1]
    head_dim = attn_weight.shape[2] // 4
    model_width = atom_feature.shape[1]
    band_width = pair_band.shape[1]
    key_count = band_width // 2
    query_count = atom_dev // win_dev
    reach = key_count - query_count
    span = key_count + reach
    span_blocks = span // query_count
    position = lax.axis_index("atoms")
    my_tokens = lax.dynamic_slice_in_dim(atom_token, position * atom_dev, atom_dev)
    band_term = jnp.einsum(
        "icz,zh->ihc",
        layer_norm(pair_band.astype(jnp.float32)),
        bias_weight,
        precision=lax.Precision.HIGHEST,
    )
    band_term = band_term.reshape(tok_dev, heads_here * band_width)

    def take_rows(carried, shard_rows, first_row):
        return select_rows(carried, shard_rows, first_row, my_tokens)

    single_init = jnp.zeros((atom_dev, trunk_single.shape[1]), jnp.bfloat16)
    band_init = jnp.zeros((atom_dev, band_term.shape[1]), jnp.float32)
    atom_rows = take_rows(single_init, trunk_single, position * tok_dev)
    atom_band = take_rows(band_init, band_term, position * tok_dev)
    for distance in range(1 - GROUP, GROUP):
        if distance != 0:
            moved_single = from_behind(trunk_single, "atoms", distance)
            moved_band = from_behind(band_term, "atoms", distance)
            source_row = (position - distance) * tok_dev
            atom_rows = take_rows(atom_rows, moved_single, source_row)
            atom_band = take_rows(atom_band, moved_band, source_row)
    atom_norm = layer_norm(atom_rows.astype(jnp.float32)).astype(jnp.bfloat16)
    token_part = jnp.dot(atom_norm, single_weight, preferred_element_type=jnp.float32).astype(
        jnp.bfloat16
    )
    atom_cond = (atom_feature.astype(jnp.float32) + token_part.astype(jnp.float32)).astype(
        jnp.bfloat16
    )
    extended = with_halo(atom_cond, (("atoms", 0),), reach)
    ext_rows = extended.shape[0]
    cond_norm = layer_norm(extended.astype(jnp.float32)).astype(jnp.bfloat16)
    projected = jnp.dot(
        cond_norm,
        attn_weight.reshape(model_width, heads_here * 4 * head_dim),
        preferred_element_type=jnp.float32,
    ).astype(jnp.bfloat16)
    projected = projected.reshape(ext_rows, heads_here, 4, head_dim)
    own_rows = projected[reach : reach + atom_dev].reshape(
        win_dev, query_count, heads_here, 4, head_dim
    )
    proj_blocks = projected.reshape(ext_rows // query_count, query_count, heads_here, 4, head_dim)
    cand_rows = jnp.stack([proj_blocks[j : j + win_dev] for j in range(span_blocks)], axis=1)
    cand_rows = cand_rows.reshape(win_dev, span, heads_here, 4, head_dim)
    padded_tok = jnp.concatenate(
        [jnp.zeros((reach,), jnp.int32), atom_token, jnp.zeros((reach,), jnp.int32)]
    )
    ext_tok = lax.dynamic_slice_in_dim(padded_tok, position * atom_dev, ext_rows).reshape(
        ext_rows // query_count, query_count
    )
    cand_tok = jnp.stack([ext_tok[j : j + win_dev] for j in range(span_blocks)], axis=1).reshape(
        win_dev, span
    )
    cand_pos = jnp.arange(span, dtype=jnp.int32)
    key_slot = cand_pos[None, :] - (key_offsets + reach)[:, None]
    in_window = (key_slot >= 0) & (key_slot < key_count)
    cand_global = (
        (jnp.arange(win_dev, dtype=jnp.int32) * query_count)[:, None]
        + cand_pos[None, :]
        - reach
        + position * atom_dev
    )
    key_valid = in_window & (cand_global >= 0) & (cand_global < total_atoms)
    query_tok = my_tokens.reshape(win_dev, query_count)
    band_index = jnp.clip(
        cand_tok[:, None, :] - query_tok[:, :, None] + key_count, 0, band_width - 1
    )
    band_rows = atom_band.reshape(win_dev, query_count, heads_here, band_width)
    column_ids = jnp.arange(band_width, dtype=jnp.int32)

    def window_bias(inputs):
        rows_here, index_here = inputs
        picker = (index_here[:, :, None] == column_ids[None, None, :]).astype(jnp.float32)
        return jnp.einsum("qhc,qrc->qhr", rows_here, picker, precision=lax.Precision.HIGHEST)

    pair_term = lax.map(window_bias, (band_rows, band_index))
    scores = (
        jnp.einsum(
            "wqhd,wrhd->wqhr",
            own_rows[:, :, :, 0],
            cand_rows[:, :, :, 1],
            preferred_element_type=jnp.float32,
        )
        / math.sqrt(head_dim)
        + pair_term
    )
    masked = jnp.where(key_valid[:, None, None, :], scores, -jnp.inf)
    row_top = jnp.max(masked, axis=-1, keepdims=True)
    exponent = jnp.exp(masked - row_top)
    weights = (exponent / jnp.sum(exponent, axis=-1, keepdims=True)).astype(jnp.bfloat16)
    attended = jnp.einsum(
        "wqhr,wrhd->wqhd", weights, cand_rows[:, :, :, 2], preferred_element_type=jnp.float32
    )
    gated_out = (jax.nn.sigmoid(own_rows[:, :, :, 3].astype(jnp.float32)) * attended).astype(
        jnp.bfloat16
    )
    gated_out = gated_out.reshape(atom_dev, heads_here * head_dim)
    partial_update = jnp.dot(gated_out, out_weight, preferred_element_type=jnp.float32)
    update = lax.psum(partial_update, "pair")
    atom_single = (atom_cond.astype(jnp.float32) + update).astype(jnp.bfloat16)
    per_atom = jax.nn.relu(jnp.dot(atom_single, token_weight, preferred_element_type=jnp.float32))

    def tally(first_row, row_count):
        relative = my_tokens - first_row
        picker = (jnp.arange(row_count, dtype=jnp.int32)[:, None] == relative[None, :]).astype(
            jnp.float32
        )
        return jnp.dot(picker, per_atom, precision=lax.Precision.HIGHEST)

    token_sums = tally(position * tok_dev, tok_dev)
    for distance in range(1 - GROUP, GROUP):
        if distance != 0:
            outgoing = tally((position + distance) * tok_dev, tok_dev)
            token_sums = token_sums + from_behind(
                outgoing.astype(jnp.bfloat16), "atoms", distance
            ).astype(outgoing.dtype)
    token_single = (token_sums / token_counts.astype(jnp.float32)[:, None]).astype(jnp.bfloat16)
    return (atom_single, token_single)


def solution(mesh):
    placed = (
        P("atoms", None),
        P("atoms", None),
        P("atoms", None, None),
        P(),
        P("atoms"),
        P("atoms"),
        P(),
        P(None, "pair", None),
        P(None, "pair"),
        P("pair", None),
        P(),
    )
    return jax.shard_map(
        shards,
        mesh=mesh,
        in_specs=placed,
        out_specs=(P("atoms", None), P("atoms", None)),
        check_vma=False,
    )
```

profile of v0, /device:TPU:24, one launch (start us, length us, event | category | flops | bytes accessed | tf_op | source)
XLA Modules:
  0.0 423.4 jit_solution(17099013851020906362)
XLA Ops:
  13.0 5.8 %collective-permute-start.2 = (bf16[96,384]{1,0:T(8,128)(2,1)}, bf16[96,384]{1,0:T(8,128)(2,1)S(1)}, u32[]{:S(2)}, u32[]{:S(2)}) collective-permute-start(bf16[96,384]{1,0:T(8,128)(2,1)} %param.13), channel_id=1, source_target_pairs={{4,0},{8,4},{12,8},{16,12},{20,16},{24,20},{28,24},{32,28},{36,32}... | collective-permute-start | bytes 221192 | tf_op jit(solution)/shard_map/ppermute | solution.py:14
  18.8 3.9 collective-permute-start.1
  26.9 4.7 %convert_reduce_fusion = f32[96,256]{1,0:T(8,128)S(1)} fusion(bf16[96,256,128]{2,1,0:T(8,128)(2,1)} %param.15), kind=kLoop, calls=%fused_computation.9 | loop fusion | flops 6266880 | bytes 6389760 | tf_op jit(solution)/shard_map/reduce_sum | solution.py:31
  31.6 7.3 %fusion.6 = f32[96,256]{1,0:T(8,128)S(1)} fusion(bf16[96,256,128]{2,1,0:T(8,128)(2,1)S(1)} %copy-done.1, f32[96,256]{1,0:T(8,128)S(1)} %broadcast_multiply_fusion), kind=kLoop, calls=%fused_computation.12 | loop fusion | flops 12558336 | bytes 6488064 | tf_op jit(solution)/shard_map/reduce_sum | solution.py:33
  39.0 17.7 %fusion.7 = f32[1,96,256]{2,0,1:T(1,128)S(1)} fusion(bf16[96,256,128]{2,1,0:T(8,128)(2,1)S(1)} %copy-done.1, f32[96,256]{1,0:T(8,128)S(1)} %add_rsqrt_fusion, f32[96,256]{1,0:T(8,128)S(1)} %broadcast_multiply_fusion, f32[128,1]{0,1:T(1,128)S(1)} %copy-done.25), kind=kOutput, calls=%fused_computation.13 | convolution fusion | flops 47185920 | bytes 6586880 | tf_op jit(solution)/shard_map/icz,zh->ihc/dot_general | solution.py:78
  59.6 6.6 %collective-permute-start = (bf16[96,384]{1,0:T(8,128)(2,1)S(1)}, bf16[96,384]{1,0:T(8,128)(2,1)S(1)}, u32[]{:S(2)}, u32[]{:S(2)}) collective-permute-start(bf16[96,384]{1,0:T(8,128)(2,1)S(1)} %copy-done.13), channel_id=1, source_target_pairs={{12,0},{16,4},{20,8},{24,12},{28,16},{32,20},{36,24},{40,28},{44,3... | collective-permute-start | bytes 221192 | tf_op jit(solution)/shard_map/ppermute | solution.py:14
  79.8 5.6 %collective-permute-start.7 = (bf16[96,128]{1,0:T(8,128)(2,1)S(1)}, bf16[96,128]{1,0:T(8,128)(2,1)S(1)}, u32[]{:S(2)}, u32[]{:S(2)}) collective-permute-start(bf16[96,128]{1,0:T(8,128)(2,1)S(1)} %get-tuple-element.70), channel_id=1, source_target_pairs={{4,0},{8,4},{12,8},{16,12},{20,16},{24,20},{28,24},{32,28},{36,32}... | collective-permute-start | bytes 73736 | tf_op jit(solution)/shard_map/ppermute | solution.py:25
  88.1 5.8 %collective-permute-start.10 = (f32[96,256]{1,0:T(8,128)S(1)}, f32[96,256]{1,0:T(8,128)S(1)}, u32[]{:S(2)}, u32[]{:S(2)}) collective-permute-start(f32[96,256]{1,0:T(8,128)S(1)} %bitcast.94), channel_id=1, source_target_pairs={{4,0},{8,4},{12,8},{16,12},{20,16},{24,20},{28,24},{32,28},{36,32}... | collective-permute-start | bytes 294920 | tf_op jit(solution)/shard_map/ppermute | solution.py:14
  117.1 5.1 %copy.21 = bf16[24,1,32,1,4,32]{2,1,5,4,0,3:T(2,128)(2,1)} copy(bf16[24,1,32,1,4,32]{5,4,2,0,3,1:T(4,128)(2,1)} %stack.50) | data formatting | bytes 393216 | tf_op jit(solution)/shard_map/stack | solution.py:120
  122.2 5.1 %copy.22 = bf16[24,1,32,1,4,32]{2,1,5,4,0,3:T(2,128)(2,1)} copy(bf16[24,1,32,1,4,32]{5,4,2,0,3,1:T(4,128)(2,1)} %stack.51) | data formatting | bytes 393216 | tf_op jit(solution)/shard_map/stack | solution.py:120
  129.4 5.1 %copy.23 = bf16[24,1,32,1,4,32]{2,1,5,4,0,3:T(2,128)(2,1)} copy(bf16[24,1,32,1,4,32]{5,4,2,0,3,1:T(4,128)(2,1)} %stack.52) | data formatting | bytes 393216 | tf_op jit(solution)/shard_map/stack | solution.py:120
  136.7 5.0 %copy.24 = bf16[24,1,32,1,4,32]{2,1,5,4,0,3:T(2,128)(2,1)} copy(bf16[24,1,32,1,4,32]{5,4,2,0,3,1:T(4,128)(2,1)} %stack.53) | data formatting | bytes 393216 | tf_op jit(solution)/shard_map/stack | solution.py:120
  143.9 5.1 %copy.25 = bf16[24,1,32,1,4,32]{2,1,5,4,0,3:T(2,128)(2,1)} copy(bf16[24,1,32,1,4,32]{5,4,2,0,3,1:T(4,128)(2,1)} %stack.54) | data formatting | bytes 393216 | tf_op jit(solution)/shard_map/stack | solution.py:120
  149.0 30.5 %stack.55 = bf16[24,7,32,1,4,32]{2,1,5,4,0,3:T(8,128)(2,1)} concatenate(bf16[24,1,32,1,4,32]{2,1,5,4,0,3:T(2,128)(2,1)S(1)} %copy.19, bf16[24,1,32,1,4,32]{2,1,5,4,0,3:T(2,128)(2,1)S(1)} %copy.20, bf16[24,1,32,1,4,32]{2,1,5,4,0,3:T(2,128)(2,1)} %copy.21, bf16[24,1,32,1,4,32]{2,1,5,4,0,3:T(2,128)(2,1)} %copy.22, bf16[24,1,32,1,4,32]{2,1,5,4,0,3:T(2,128)(2,1)} %copy.23, ...), dimensions={1} | concatenate | bytes 2752512 | tf_op jit(solution)/shard_map/stack | solution.py:120
  179.4 8.4 %reshape.287 = bf16[24,224,1,4,32]{1,4,3,0,2:T(8,128)(2,1)} reshape(bf16[24,7,32,1,4,32]{2,1,5,4,0,3:T(8,128)(2,1)} %stack.55) | data formatting | bytes 2752512 | tf_op jit(solution)/shard_map/reshape | solution.py:121
  190.5 143.8 %while.11 = (s32[]{:T(128)}, f32[24,32,1,224]{3,1,0,2:T(8,128)}, f32[24,32,1,256]{3,1,0,2:T(8,128)}, s32[24,32,224]{2,1,0:T(8,128)}, s32[]{:T(128)}) while((s32[]{:T(128)}, f32[24,32,1,224]{3,1,0,2:T(8,128)}, f32[24,32,1,256]{3,1,0,2:T(8,128)}, s32[24,32,224]{2,1,0:T(8,128)}, s32[]{:T(128)}) %tuple.55), condition=%wide.region_7.8_spmd.clone, body=%wide.region_6.7_spmd.clone.sunk | while | flops 23855104 | bytes 275013 | solution.py:153
  192.1 3.8 fusion.112
  198.1 3.8 fusion.112
  204.1 3.8 fusion.112
  210.1 3.8 fusion.112
  216.1 3.8 fusion.112
  222.1 3.8 fusion.112
  228.1 3.8 fusion.112
  234.1 3.8 fusion.112
  240.1 3.8 fusion.112
  246.1 3.8 fusion.112
  252.0 3.8 fusion.112
  258.0 3.8 fusion.112
  264.0 3.8 fusion.112
  270.0 3.8 fusion.112
  338.2 46.2 %all-reduce.2.cloned.1.call-done = f32[768,128]{1,0:T(8,128)} async-done(((f32[768,128]{1,0:T(8,128)}), f32[768,128]{1,0:T(8,128)}) %all-reduce.2.cloned.1.call-update) | async-done | bytes 393232 | tf_op jit(solution)/shard_map/psum | solution.py:176
  396.9 4.1 collective-permute-start.16
  (251 shorter events, 182.8 us)
Async XLA Ops:
  7.2 378.3 %copy-start = (bf16[128,384]{1,0:T(8,128)(2,1)S(1)}, bf16[128,384]{1,0:T(8,128)(2,1)}, u32[]{:S(2)}) copy-start(bf16[128,384]{1,0:T(8,128)(2,1)} %param.23) | copy-start | bytes 294916
  7.2 377.2 %all-reduce.2.cloned.1.call-start = ((), (), s32[]{:S(2)}) async-start(), calls=%async_computation | async-start | bytes 786432 | tf_op jit(solution)/shard_map/psum | solution.py:176
  7.2 52.4 %collective-permute-start.4 = (bf16[96,384]{1,0:T(8,128)(2,1)}, bf16[96,384]{1,0:T(8,128)(2,1)S(1)}, u32[]{:S(2)}, u32[]{:S(2)}) collective-permute-start(bf16[96,384]{1,0:T(8,128)(2,1)} %param.13), channel_id=1, source_target_pairs={{0,8},{4,12},{8,16},{12,20},{16,24},{20,28},{24,32},{28,36},{32,40... | collective-permute-start | bytes 221192 | tf_op jit(solution)/shard_map/ppermute | solution.py:14
  11.1 55.7 %collective-permute-start.3 = (bf16[96,384]{1,0:T(8,128)(2,1)}, bf16[96,384]{1,0:T(8,128)(2,1)S(1)}, u32[]{:S(2)}, u32[]{:S(2)}) collective-permute-start(bf16[96,384]{1,0:T(8,128)(2,1)} %param.13), channel_id=1, source_target_pairs={{0,4},{4,8},{8,12},{12,16},{16,20},{20,24},{24,28},{28,32},{32,36}... | collective-permute-start | bytes 221192 | tf_op jit(solution)/shard_map/ppermute | solution.py:14
  13.0 56.2 %collective-permute-start.2 = (bf16[96,384]{1,0:T(8,128)(2,1)}, bf16[96,384]{1,0:T(8,128)(2,1)S(1)}, u32[]{:S(2)}, u32[]{:S(2)}) collective-permute-start(bf16[96,384]{1,0:T(8,128)(2,1)} %param.13), channel_id=1, source_target_pairs={{4,0},{8,4},{12,8},{16,12},{20,16},{24,20},{28,24},{32,28},{36,32}... | collective-permute-start | bytes 221192 | tf_op jit(solution)/shard_map/ppermute | solution.py:14
  18.8 54.6 %collective-permute-start.1 = (bf16[96,384]{1,0:T(8,128)(2,1)}, bf16[96,384]{1,0:T(8,128)(2,1)S(1)}, u32[]{:S(2)}, u32[]{:S(2)}) collective-permute-start(bf16[96,384]{1,0:T(8,128)(2,1)} %param.13), channel_id=1, source_target_pairs={{8,0},{12,4},{16,8},{20,12},{24,16},{28,20},{32,24},{36,28},{40,32... | collective-permute-start | bytes 221192 | tf_op jit(solution)/shard_map/ppermute | solution.py:14
  22.7 53.1 %collective-permute-start.5 = (bf16[96,384]{1,0:T(8,128)(2,1)}, bf16[96,384]{1,0:T(8,128)(2,1)S(1)}, u32[]{:S(2)}, u32[]{:S(2)}) collective-permute-start(bf16[96,384]{1,0:T(8,128)(2,1)} %param.13), channel_id=1, source_target_pairs={{0,12},{4,16},{8,20},{12,24},{16,28},{20,32},{24,36},{28,40},{32,4... | collective-permute-start | bytes 221192 | tf_op jit(solution)/shard_map/ppermute | solution.py:14
  25.4 72.9 %copy-start.16 = (s32[768]{0:T(1024)}, s32[768]{0:T(1024)S(1)}, u32[]{:S(2)}) copy-start(s32[768]{0:T(1024)S(1)} %get-tuple-element.58) | copy-start | bytes 9220
  25.5 49.8 %copy-start.18 = (s32[768]{0:T(1024)}, s32[768]{0:T(1024)S(1)}, u32[]{:S(2)}) copy-start(s32[768]{0:T(1024)S(1)} %get-tuple-element.83) | copy-start | bytes 9220
  25.5 76.0 %copy-start.14 = (s32[768]{0:T(1024)}, s32[768]{0:T(1024)S(1)}, u32[]{:S(2)}) copy-start(s32[768]{0:T(1024)S(1)} %get-tuple-element.79) | copy-start | bytes 9220
  39.0 18.3 %copy-start.11 = (s32[49152]{0:T(1024)S(1)}, s32[49152]{0:T(1024)}, u32[]{:S(2)}) copy-start(s32[49152]{0:T(1024)} %param.16) | copy-start | bytes 589828
  59.6 16.7 %collective-permute-start = (bf16[96,384]{1,0:T(8,128)(2,1)S(1)}, bf16[96,384]{1,0:T(8,128)(2,1)S(1)}, u32[]{:S(2)}, u32[]{:S(2)}) collective-permute-start(bf16[96,384]{1,0:T(8,128)(2,1)S(1)} %copy-done.13), channel_id=1, source_target_pairs={{12,0},{16,4},{20,8},{24,12},{28,16},{32,20},{36,24},{40,28},{44,3... | collective-permute-start | bytes 221192 | tf_op jit(solution)/shard_map/ppermute | solution.py:14
  66.8 29.4 %collective-permute-start.8 = (f32[96,256]{1,0:T(8,128)S(1)}, f32[96,256]{1,0:T(8,128)S(1)}, u32[]{:S(2)}, u32[]{:S(2)}) collective-permute-start(f32[96,256]{1,0:T(8,128)S(1)} %bitcast.90), channel_id=1, source_target_pairs={{12,0},{16,4},{20,8},{24,12},{28,16},{32,20},{36,24},{40,28},{44,3... | collective-permute-start | bytes 294920 | tf_op jit(solution)/shard_map/ppermute | solution.py:14
  69.2 32.3 %collective-permute-start.13 = (f32[96,256]{1,0:T(8,128)S(1)}, f32[96,256]{1,0:T(8,128)S(1)}, u32[]{:S(2)}, u32[]{:S(2)}) collective-permute-start(f32[96,256]{1,0:T(8,128)S(1)} %bitcast.91), channel_id=1, source_target_pairs={{0,12},{4,16},{8,20},{12,24},{16,28},{20,32},{24,36},{28,40},{32,4... | collective-permute-start | bytes 294920 | tf_op jit(solution)/shard_map/ppermute | solution.py:14
  73.3 29.6 %collective-permute-start.12 = (f32[96,256]{1,0:T(8,128)S(1)}, f32[96,256]{1,0:T(8,128)S(1)}, u32[]{:S(2)}, u32[]{:S(2)}) collective-permute-start(f32[96,256]{1,0:T(8,128)S(1)} %bitcast.92), channel_id=1, source_target_pairs={{0,8},{4,12},{8,16},{12,20},{16,24},{20,28},{24,32},{28,36},{32,40... | collective-permute-start | bytes 294920 | tf_op jit(solution)/shard_map/ppermute | solution.py:14
  77.4 17.1 %copy-start.24 = (bf16[128,1,128]{2,0,1:T(8,128)(2,1)S(1)}, bf16[128,1,128]{2,0,1:T(8,128)(2,1)}, u32[]{:S(2)}) copy-start(bf16[128,1,128]{2,0,1:T(8,128)(2,1)} %param.20) | copy-start | bytes 98308
  77.8 8.4 %collective-permute-start.6 = (bf16[96,128]{1,0:T(8,128)(2,1)S(1)}, bf16[96,128]{1,0:T(8,128)(2,1)S(1)}, u32[]{:S(2)}, u32[]{:S(2)}) collective-permute-start(bf16[96,128]{1,0:T(8,128)(2,1)S(1)} %get-tuple-element.69), channel_id=1, source_target_pairs={{0,4},{4,8},{8,12},{12,16},{16,20},{20,24},{24,28},{28,32},{32,36}... | collective-permute-start | bytes 73736 | tf_op jit(solution)/shard_map/ppermute | solution.py:22
  79.8 8.2 %collective-permute-start.7 = (bf16[96,128]{1,0:T(8,128)(2,1)S(1)}, bf16[96,128]{1,0:T(8,128)(2,1)S(1)}, u32[]{:S(2)}, u32[]{:S(2)}) collective-permute-start(bf16[96,128]{1,0:T(8,128)(2,1)S(1)} %get-tuple-element.70), channel_id=1, source_target_pairs={{4,0},{8,4},{12,8},{16,12},{20,16},{24,20},{28,24},{32,28},{36,32}... | collective-permute-start | bytes 73736 | tf_op jit(solution)/shard_map/ppermute | solution.py:25
  86.2 18.2 %collective-permute-start.11 = (f32[96,256]{1,0:T(8,128)S(1)}, f32[96,256]{1,0:T(8,128)S(1)}, u32[]{:S(2)}, u32[]{:S(2)}) collective-permute-start(f32[96,256]{1,0:T(8,128)S(1)} %bitcast.93), channel_id=1, source_target_pairs={{0,4},{4,8},{8,12},{12,16},{16,20},{20,24},{24,28},{28,32},{32,36}... | collective-permute-start | bytes 294920 | tf_op jit(solution)/shard_map/ppermute | solution.py:14
  88.1 17.7 %collective-permute-start.10 = (f32[96,256]{1,0:T(8,128)S(1)}, f32[96,256]{1,0:T(8,128)S(1)}, u32[]{:S(2)}, u32[]{:S(2)}) collective-permute-start(f32[96,256]{1,0:T(8,128)S(1)} %bitcast.94), channel_id=1, source_target_pairs={{4,0},{8,4},{12,8},{16,12},{20,16},{24,20},{28,24},{32,28},{36,32}... | collective-permute-start | bytes 294920 | tf_op jit(solution)/shard_map/ppermute | solution.py:14
  96.2 91.6 %collective-permute-start.9 = (f32[96,256]{1,0:T(8,128)S(1)}, f32[96,256]{1,0:T(8,128)}, u32[]{:S(2)}, u32[]{:S(2)}) collective-permute-start(f32[96,256]{1,0:T(8,128)S(1)} %bitcast.95), channel_id=1, source_target_pairs={{8,0},{12,4},{16,8},{20,12},{24,16},{28,20},{32,24},{36,28},{40,32... | collective-permute-start | bytes 294920 | tf_op jit(solution)/shard_map/ppermute | solution.py:14
  190.5 143.8 %copy-start.7 = (bf16[24,32,1,1,32]{4,3,1,0,2:T(2,128)(2,1)S(1)}, bf16[24,32,1,1,32]{4,3,1,0,2:T(2,128)(2,1)}, u32[]{:S(2)}) copy-start(bf16[24,32,1,1,32]{4,3,1,0,2:T(2,128)(2,1)} %get-tuple-element.60) | copy-start | bytes 147460
  190.5 144.8 %copy-start.6 = (bf16[24,224,1,4,32]{1,4,3,0,2:T(8,128)(2,1)S(1)}, bf16[24,224,1,4,32]{1,4,3,0,2:T(8,128)(2,1)}, u32[]{:S(2)}) copy-start(bf16[24,224,1,4,32]{1,4,3,0,2:T(8,128)(2,1)} %reshape.287) | copy-start | bytes 4128772
  190.5 144.8 %copy-start.8 = (bf16[24,32,1,1,32]{4,3,1,0,2:T(2,128)(2,1)S(1)}, bf16[24,32,1,1,32]{4,3,1,0,2:T(2,128)(2,1)}, u32[]{:S(2)}) copy-start(bf16[24,32,1,1,32]{4,3,1,0,2:T(2,128)(2,1)} %get-tuple-element.61) | copy-start | bytes 147460
  338.2 47.6 %copy-start.15 = (s32[768]{0:T(1024)S(1)}, s32[768]{0:T(1024)}, u32[]{:S(2)}) copy-start(s32[768]{0:T(1024)} %copy-done.14) | copy-start | bytes 9220
  388.3 19.6 %copy-start.27 = (s32[96]{0:T(128)S(1)}, s32[96]{0:T(128)}, u32[]{:S(2)}) copy-start(s32[96]{0:T(128)} %param.17) | copy-start | bytes 1156
  388.9 16.6 %collective-permute-start.14 = (bf16[96,384]{1,0:T(8,128)(2,1)S(1)}, bf16[96,384]{1,0:T(8,128)(2,1)S(1)}, u32[]{:S(2)}, u32[]{:S(2)}) collective-permute-start(bf16[96,384]{1,0:T(8,128)(2,1)S(1)} %convolution_convert_fusion.14), channel_id=1, source_target_pairs={{12,0},{16,4},{20,8},{24,12},{28,16},{32,20},{36,24},{40,28},{44,3... | collective-permute-start | bytes 221192 | tf_op jit(solution)/shard_map/ppermute | solution.py:14
  393.1 14.7 %collective-permute-start.15 = (bf16[96,384]{1,0:T(8,128)(2,1)S(1)}, bf16[96,384]{1,0:T(8,128)(2,1)S(1)}, u32[]{:S(2)}, u32[]{:S(2)}) collective-permute-start(bf16[96,384]{1,0:T(8,128)(2,1)S(1)} %convolution_convert_fusion.13), channel_id=1, source_target_pairs={{8,0},{12,4},{16,8},{20,12},{24,16},{28,20},{32,24},{36,28},{40,32... | collective-permute-start | bytes 221192 | tf_op jit(solution)/shard_map/ppermute | solution.py:14
  396.9 10.9 %collective-permute-start.16 = (bf16[96,384]{1,0:T(8,128)(2,1)S(1)}, bf16[96,384]{1,0:T(8,128)(2,1)S(1)}, u32[]{:S(2)}, u32[]{:S(2)}) collective-permute-start(bf16[96,384]{1,0:T(8,128)(2,1)S(1)} %convolution_convert_fusion.12), channel_id=1, source_target_pairs={{4,0},{8,4},{12,8},{16,12},{20,16},{24,20},{28,24},{32,28},{36,32}... | collective-permute-start | bytes 221192 | tf_op jit(solution)/shard_map/ppermute | solution.py:14
  401.0 7.8 %collective-permute-start.17 = (bf16[96,384]{1,0:T(8,128)(2,1)S(1)}, bf16[96,384]{1,0:T(8,128)(2,1)S(1)}, u32[]{:S(2)}, u32[]{:S(2)}) collective-permute-start(bf16[96,384]{1,0:T(8,128)(2,1)S(1)} %convolution_convert_fusion.11), channel_id=1, source_target_pairs={{0,4},{4,8},{8,12},{12,16},{16,20},{20,24},{24,28},{28,32},{32,36}... | collective-permute-start | bytes 221192 | tf_op jit(solution)/shard_map/ppermute | solution.py:14
  402.9 8.9 %collective-permute-start.18 = (bf16[96,384]{1,0:T(8,128)(2,1)S(1)}, bf16[96,384]{1,0:T(8,128)(2,1)S(1)}, u32[]{:S(2)}, u32[]{:S(2)}) collective-permute-start(bf16[96,384]{1,0:T(8,128)(2,1)S(1)} %convolution_convert_fusion.10), channel_id=1, source_target_pairs={{0,8},{4,12},{8,16},{12,20},{16,24},{20,28},{24,32},{28,36},{32,40... | collective-permute-start | bytes 221192 | tf_op jit(solution)/shard_map/ppermute | solution.py:14
  405.5 9.7 %collective-permute-start.19 = (bf16[96,384]{1,0:T(8,128)(2,1)S(1)}, bf16[96,384]{1,0:T(8,128)(2,1)S(1)}, u32[]{:S(2)}, u32[]{:S(2)}) collective-permute-start(bf16[96,384]{1,0:T(8,128)(2,1)S(1)} %convolution_convert_fusion.9), channel_id=1, source_target_pairs={{0,12},{4,16},{8,20},{12,24},{16,28},{20,32},{24,36},{28,40},{32,4... | collective-permute-start | bytes 221192 | tf_op jit(solution)/shard_map/ppermute | solution.py:14
  (17 other events, 64.2 us)
Sparse Core Ops, SparseCore 0:
  338.3 46.0 all-reduce.1
where the time goes:
time: 432 us; the launch traced here: 423 us
  local copies, waits for them, and re-layouts  138 us (32%)
  matrix products  132 us (31%)
  starting transfers between devices  67.2 us (16%)
  waiting for transfers between devices  53.7 us (12%)
  other arithmetic  16.9 us (4%)
  between operations  14.9 us (3%)
    dot_general x24, matrix products, window_bias(): jnp.einsum('qhc,qrc->qhr', rows_here, picker, precision=lax.Precision.HIG...  92.2 us
    another operation x15, local copies, waits for them, and re-layouts, shards(): jnp.stack([proj_blocks[j:j + win_dev] for j in range(span_blocks)], axis=1)  72.2 us
    ppermute x18, starting transfers between devices, from_behind(): lax.ppermute(value, axis, [(source, source + steps) for source in range(l...  59.5 us
    psum x1, waiting for transfers between devices, shards(): update = lax.psum(partial_update, 'pair')  46.2 us
    dynamic_slice x24, local copies, waits for them, and re-layouts, shards(): pair_term = lax.map(window_bias, (band_rows, band_index))  18.4 us
    eq x24, local copies, waits for them, and re-layouts, window_bias(): index_here[:, :, None] == column_ids[None, None, :]  18.2 us
    dot_general x1, matrix products, shards(): jnp.einsum('icz,zh->ihc', layer_norm(pair_band.astype(jnp.float32)), bias...  17.7 us
    dynamic_update_slice x24, local copies, waits for them, and re-layouts, shards(): pair_term = lax.map(window_bias, (band_rows, band_index))  15 us
  transfers between devices with their start and end apart: 21, of which 4 were waited for; matrix products, arithmetic and copies ran while one was open for 31% of the time, Pallas kernels for 0%

commit v1 on v0

v1 whole, which is shorter than its diff:
```python
import functools
import math

import jax
import jax.numpy as jnp
from jax import lax
from jax.experimental import pallas as pl
from jax.experimental.pallas import tpu as pltpu
from jax.sharding import PartitionSpec as P

GROUP = 4
LANES = 128
MESH = pl.DeviceIdType.MESH
F32 = jnp.float32
BF16 = jnp.bfloat16
CHUNKS = 4
NT = (((1,), (1,)), ((), ()))


def dot(a, b):
    return jnp.dot(a, b, preferred_element_type=F32)


def norm_rows(x):
    centred = x - jnp.mean(x, axis=-1, keepdims=True)
    spread = jnp.mean(centred * centred, axis=-1, keepdims=True)
    return centred * lax.rsqrt(spread + 1e-05)


def kernel(
    sizes,
    trunk, feat, band, tok, counts, koff, single_w, attn_w, bias_w, out_w, token_w,
    atom_out, token_out,
    band_v, tp_all, bias_all, cond, proj, qs, gate, onehot, onehot_t, tokq, tokl,
    ow_all, ow_cat, bias_hi, bias_lo, packed, atoms_bf, sums, sums_out, sums_in,
    band_sem, tp_send, tp_recv, ow_send, ow_recv, bias_send, bias_recv,
    halo_send, halo_recv, gate_send, gate_recv, sum_send, sum_recv,
):
    n_dev, n_pair, total_atoms = sizes
    tok_dev = trunk.shape[0]
    atom_dev = feat.shape[0]
    blocks = atom_dev // LANES
    reach = 96
    query_count = 32
    group_tok = GROUP * tok_dev
    part = tok_dev // CHUNKS
    a = lax.axis_index("atoms")
    p = lax.axis_index("pair")
    r = lax.rem(a, GROUP)
    base = a - r
    left = lax.rem(a + n_dev - 1, n_dev)
    right = lax.rem(a + 1, n_dev)

    def group_peer(d):
        return (base + lax.rem(r + d, GROUP), p)

    def pair_peer(d):
        return (a, lax.rem(p + d, n_pair))

    barrier = pltpu.get_barrier_semaphore()
    for d in range(1, GROUP):
        pl.semaphore_signal(barrier, inc=1, device_id=group_peer(d), device_id_type=MESH)
    for d in range(1, n_pair):
        pl.semaphore_signal(barrier, inc=1, device_id=pair_peer(d), device_id_type=MESH)
    pl.semaphore_signal(barrier, inc=1, device_id=(left, p), device_id_type=MESH)
    pl.semaphore_signal(barrier, inc=1, device_id=(right, p), device_id_type=MESH)

    def band_copy(c):
        rows = pl.ds(c * part, part)
        return pltpu.make_async_copy(band.at[rows], band_v.at[rows], band_sem.at[c])

    for c in range(CHUNKS):
        band_copy(c).start()

    def remote(src, dst, send, recv, device):
        return pltpu.make_async_remote_copy(
            src_ref=src, dst_ref=dst, send_sem=send, recv_sem=recv, device_id=device, device_id_type=MESH
        )

    def tp_copy(d):
        return remote(tp_all.at[r], tp_all.at[r], tp_send.at[d], tp_recv.at[d], group_peer(d))

    def tp_arrive(d):
        s = lax.rem(r + GROUP - d, GROUP)
        return remote(tp_all.at[s], tp_all.at[s], tp_send.at[d], tp_recv.at[d], group_peer(d))

    def ow_copy(d):
        return remote(ow_all.at[p], ow_all.at[p], ow_send.at[d], ow_recv.at[d], pair_peer(d))

    def ow_arrive(d):
        s = lax.rem(p + n_pair - d, n_pair)
        return remote(ow_all.at[s], ow_all.at[s], ow_send.at[d], ow_recv.at[d], pair_peer(d))

    def bias_copy(c, d):
        rows = pl.ds(c * part, part)
        return remote(
            bias_all.at[r, rows], bias_all.at[r, rows], bias_send.at[c, d], bias_recv.at[c, d], group_peer(d)
        )

    def bias_arrive(c, d):
        s = lax.rem(r + GROUP - d, GROUP)
        rows = pl.ds(c * part, part)
        return remote(
            bias_all.at[s, rows], bias_all.at[s, rows], bias_send.at[c, d], bias_recv.at[c, d], group_peer(d)
        )

    first, last = LANES, LANES + atom_dev

    def to_right():
        return remote(
            cond.at[pl.ds(last - reach, reach)], cond.at[pl.ds(first - reach, reach)],
            halo_send.at[0], halo_recv.at[0], (right, p),
        )

    def to_left():
        return remote(
            cond.at[pl.ds(first, reach)], cond.at[pl.ds(last, reach)],
            halo_send.at[1], halo_recv.at[1], (left, p),
        )

    def gate_copy(b, d):
        rows = pl.ds(b * query_count, query_count)
        return remote(
            packed.at[p, rows], packed.at[p, rows], gate_send.at[b, d], gate_recv.at[b, d], pair_peer(d)
        )

    def gate_arrive(b, d):
        s = lax.rem(p + n_pair - d, n_pair)
        rows = pl.ds(b * query_count, query_count)
        return remote(
            packed.at[s, rows], packed.at[s, rows], gate_send.at[b, d], gate_recv.at[b, d], pair_peer(d)
        )

    def sum_copy(d):
        t = lax.rem(r + d, GROUP)
        return remote(sums_out.at[t], sums_in.at[d], sum_send.at[d], sum_recv.at[d], group_peer(d))

    tp_all[r] = dot(norm_rows(trunk[...].astype(F32)).astype(BF16), single_w[...]).astype(BF16)
    ow_all[p] = out_w[...]
    for i in range(blocks + 2):
        row = lax.rem(a * blocks + i - 1 + total_atoms // LANES, total_atoms // LANES)
        tokl[i : i + 1, :] = tok[pl.ds(row, 1), :]

    pl.semaphore_wait(barrier, 3 + n_pair - 1 + 2)
    for d in range(1, GROUP):
        tp_copy(d).start()
    for d in range(1, n_pair):
        ow_copy(d).start()

    w = bias_w[...]
    w_hi = w.astype(BF16).astype(F32)
    w_mid = (w - w_hi).astype(BF16).astype(F32)
    w_lo = w - w_hi - w_mid
    w_total = jnp.sum(w, axis=1, keepdims=True)
    row_id = lax.broadcasted_iota(jnp.int32, (16, LANES), 0)
    parts = jnp.where(
        row_id == 0, w_hi, jnp.where(row_id == 1, w_mid, jnp.where(row_id == 2, w_lo, jnp.where(row_id == 3, 1.0, 0.0)))
    ).astype(BF16)
    lane8 = lax.broadcasted_iota(jnp.int32, (8, LANES), 1)
    diag_mask = lax.rem(lane8, 8) == lax.broadcasted_iota(jnp.int32, (8, LANES), 0)
    lane_group = lane8 // 8

    def band_rows(x):
        g = lax.dot_general(jnp.concatenate([x, parts], axis=0), x, NT, preferred_element_type=F32)
        acc = g[0:8]
        for s in range(1, LANES // 8):
            acc = jnp.where(lane_group == s, g[8 * s : 8 * s + 8], acc)
        squares = jnp.sum(jnp.where(diag_mask, acc, 0.0), axis=0, keepdims=True)
        products = g[LANES : LANES + 1] + g[LANES + 1 : LANES + 2] + g[LANES + 2 : LANES + 3]
        return products, g[LANES + 3 : LANES + 4], squares

    def band_step(start):
        halves = []
        for half in range(2):
            got = [band_rows(band_v[start + t, half * LANES : (half + 1) * LANES, :]) for t in range(8)]
            products, total, squares = (jnp.concatenate(list(v), axis=0) for v in zip(*got))
            mean = total * (1.0 / LANES)
            spread = jnp.maximum(squares * (1.0 / LANES) - mean * mean, 0.0)
            halves.append((products - mean * w_total) * lax.rsqrt(spread + 1e-05))
        bias_all[r, pl.ds(pl.multiple_of(start, 8), 8), :] = jnp.concatenate(halves, axis=1)

    def band_chunk(c, carry):
        band_copy(c).wait()

        def step(i, inner):
            band_step(c * part + i * 8)
            return inner

        lax.fori_loop(0, part // 8, step, 0)
        for d in range(1, GROUP):
            bias_copy(c, d).start()
        return carry

    lax.fori_loop(0, CHUNKS // 2, band_chunk, 0)

    token_base = (base * tok_dev).astype(jnp.int32)
    for d in range(1, GROUP):
        tp_arrive(d).wait_recv()
    cond[0 : first - reach, :] = jnp.zeros((first - reach, LANES), BF16)
    cond[last + reach : last + LANES, :] = jnp.zeros((LANES - reach, LANES), BF16)

    def cond_block(b, carry):
        rows = pl.ds(pl.multiple_of(b * LANES, LANES), LANES)
        tok_row = tokl[pl.ds(b + 1, 1), :] - token_base
        spread_row = jnp.broadcast_to(tok_row, (LANES, LANES))
        tok_col = spread_row.astype(F32).T.astype(jnp.int32)
        tokq[rows, :] = tok_col + token_base
        lane = lax.broadcasted_iota(jnp.int32, (LANES, LANES), 1)
        pick = jnp.concatenate(
            [(tok_col == lane + k * LANES).astype(F32).astype(BF16) for k in range(group_tok // LANES)], axis=1
        )
        onehot[rows, :] = pick
        sub = lax.broadcasted_iota(jnp.int32, (group_tok, LANES), 0)
        onehot_t[b] = (jnp.broadcast_to(tok_row, (group_tok, LANES)) == sub).astype(F32).astype(BF16)
        chosen = dot(pick, tp_all[...].reshape(group_tok, LANES)).astype(BF16)
        cond[pl.ds(pl.multiple_of(first + b * LANES, LANES), LANES), :] = (
            feat[rows, :].astype(F32) + chosen.astype(F32)
        ).astype(BF16)
        return carry

    lax.fori_loop(0, blocks, cond_block, 0)
    to_right().start()
    to_left().start()

    lax.fori_loop(CHUNKS // 2, CHUNKS, band_chunk, 0)

    lane1 = lax.broadcasted_iota(jnp.int32, (LANES, LANES), 1)
    aw = attn_w[...]
    aw32 = aw.astype(F32)
    head = lane1 // 32
    q_w = jnp.where(head == 1, pltpu.roll(aw32, 32, 1), 0.0).astype(BF16)
    g_w = jnp.where(head == 2, pltpu.roll(aw32, LANES - 32, 1), 0.0).astype(BF16)

    def proj_block(b, carry):
        rows = pl.ds(pl.multiple_of(b * LANES, LANES), LANES)
        ext = pl.ds(pl.multiple_of(first + b * LANES, LANES), LANES)
        normed = norm_rows(cond[ext, :].astype(F32)).astype(BF16)
        proj[ext, :] = dot(normed, aw).astype(BF16)
        qs[rows, :] = dot(normed, q_w).astype(BF16)
        gate[rows, :] = jax.nn.sigmoid(dot(normed, g_w).astype(BF16).astype(F32))
        return carry

    lax.fori_loop(0, blocks, proj_block, 0)
    to_right().wait_recv()
    to_left().wait_recv()
    for start in (0, last):
        normed = norm_rows(cond[start : start + LANES, :].astype(F32)).astype(BF16)
        proj[start : start + LANES, :] = dot(normed, aw).astype(BF16)

    for d in range(1, n_pair):
        ow_arrive(d).wait_recv()
    ow_cat[...] = jnp.zeros(ow_cat.shape, BF16)
    for h in range(n_pair):
        for j in range(4):
            ow_cat[h * LANES + 32 * j : h * LANES + 32 * j + 32, j * LANES : (j + 1) * LANES] = ow_all[h]

    def wait_bias(c, carry):
        for d in range(1, GROUP):
            bias_arrive(c, d).wait_recv()
        return carry

    lax.fori_loop(0, CHUNKS, wait_bias, 0)
    for s in range(GROUP):
        whole = bias_all[s]
        high = whole.astype(BF16)
        bias_hi[s] = high
        bias_lo[s] = (whole - high.astype(F32)).astype(BF16)

    width = 3 * LANES

    def attend(b, carry):
        rows = pl.ds(pl.multiple_of(b * LANES, LANES), LANES)
        keys = proj[pl.ds(pl.multiple_of(b * LANES, LANES), width), :]
        raw = lax.dot_general(qs[rows, :], keys, NT, preferred_element_type=F32) * (1.0 / math.sqrt(32.0))
        pick = onehot[rows, :]
        mine = dot(pick, bias_hi[...].reshape(group_tok, 2 * LANES)) + dot(
            pick, bias_lo[...].reshape(group_tok, 2 * LANES)
        )
        low, high = mine[:, :LANES], mine[:, LANES:]
        my_tok = tokq[rows, :]
        sub = lax.broadcasted_iota(jnp.int32, (LANES, LANES), 0)
        window = sub // query_count
        offset = jnp.where(
            window == 0,
            koff[4 * b],
            jnp.where(window == 1, koff[4 * b + 1], jnp.where(window == 2, koff[4 * b + 2], koff[4 * b + 3])),
        )
        shift = offset + window * query_count
        pieces = []
        for t in range(3):
            index = tokl[pl.ds(b + t, 1), :] - my_tok + LANES
            wrapped = index & (LANES - 1)
            first_half = jnp.take_along_axis(low, wrapped, axis=1, mode="promise_in_bounds")
            second_half = jnp.take_along_axis(high, wrapped, axis=1, mode="promise_in_bounds")
            value = raw[:, t * LANES : (t + 1) * LANES] + jnp.where(index >= LANES, second_half, first_half)
            slot = lane1 + (t - 1) * LANES - shift
            place = lane1 + (a * atom_dev + (b + t - 1) * LANES)
            valid = (slot >= 0) & (slot < LANES) & (place >= 0) & (place < total_atoms)
            pieces.append(jnp.where(valid, value, -jnp.inf))
        masked = jnp.concatenate(pieces, axis=1)
        top = jnp.max(masked, axis=1, keepdims=True)
        exponent = jnp.exp(masked - top)
        weights = (exponent / jnp.sum(exponent, axis=1, keepdims=True)).astype(BF16)
        gated = gate[rows, :] * dot(weights, keys)
        lane32 = lax.broadcasted_iota(jnp.int32, (query_count, LANES), 1) // 32
        out = jnp.zeros((query_count, LANES), F32)
        for j in range(4):
            turned = pltpu.roll(gated[32 * j : 32 * j + 32], (32 * j + 64) % LANES, 1)
            out = jnp.where(lane32 == j, turned, out)
        packed[p, pl.ds(pl.multiple_of(b * query_count, 32), query_count), :] = out.astype(BF16)
        for d in range(1, n_pair):
            gate_copy(b, d).start()
        return carry

    lax.fori_loop(0, blocks, attend, 0)

    def wait_gate(b, carry):
        for d in range(1, n_pair):
            gate_arrive(b, d).wait_recv()
        return carry

    lax.fori_loop(0, blocks, wait_gate, 0)

    update = dot(packed[0], ow_cat[0:LANES, :])
    for h in range(1, n_pair):
        update = update + dot(packed[h], ow_cat[h * LANES : (h + 1) * LANES, :])
    for b in range(blocks):
        for j in range(4):
            at = b * LANES + 32 * j
            value = cond[first + at : first + at + 32, :].astype(F32) + update[
                32 * b : 32 * b + 32, j * LANES : (j + 1) * LANES
            ]
            atoms_bf[at : at + 32, :] = value.astype(BF16)
    atom_out[...] = atoms_bf[...]
    total = None
    for b in range(blocks):
        per_atom = jnp.maximum(dot(atoms_bf[b * LANES : (b + 1) * LANES, :], token_w[...]), 0.0).astype(BF16)
        term = dot(onehot_t[b], per_atom)
        total = term if total is None else total + term
    for s in range(GROUP):
        sums[s] = total[s * tok_dev : (s + 1) * tok_dev]
        sums_out[s] = total[s * tok_dev : (s + 1) * tok_dev].astype(BF16)
    for d in range(1, GROUP):
        sum_copy(d).start()
    eye = lax.broadcasted_iota(jnp.int32, (tok_dev, tok_dev), 0) == lax.broadcasted_iota(
        jnp.int32, (tok_dev, tok_dev), 1
    )
    count = jnp.sum(jnp.where(eye, counts[...].astype(F32), 0.0), axis=1, keepdims=True)
    result = sums[r]
    for d in range(1, GROUP):
        sum_copy(d).wait_recv()
        result = result + sums_in[d].astype(F32)
    token_out[...] = (result / count).astype(BF16)

    for d in range(1, GROUP):
        tp_copy(d).wait_send()
        sum_copy(d).wait_send()
    for d in range(1, n_pair):
        ow_copy(d).wait_send()
    to_right().wait_send()
    to_left().wait_send()

    def drain_bias(c, carry):
        for d in range(1, GROUP):
            bias_copy(c, d).wait_send()
        return carry

    lax.fori_loop(0, CHUNKS, drain_bias, 0)

    def drain_gate(b, carry):
        for d in range(1, n_pair):
            gate_copy(b, d).wait_send()
        return carry

    lax.fori_loop(0, blocks, drain_gate, 0)


def shards(
    trunk_single, atom_feature, pair_band, atom_token, token_counts, key_offsets,
    single_weight, attn_weight, bias_weight, out_weight, token_weight,
):
    n_dev = lax.axis_size("atoms")
    n_pair = lax.axis_size("pair")
    tok_dev, width = trunk_single.shape
    atom_dev = atom_feature.shape[0]
    blocks = atom_dev // LANES
    total_atoms = atom_token.shape[0]
    group_tok = GROUP * tok_dev
    ext = atom_dev + 2 * LANES
    vmem = pl.BlockSpec(memory_space=pltpu.VMEM)
    dma = pltpu.SemaphoreType.DMA
    return pl.pallas_call(
        functools.partial(kernel, (n_dev, n_pair, total_atoms)),
        out_shape=(
            jax.ShapeDtypeStruct((atom_dev, LANES), BF16),
            jax.ShapeDtypeStruct((tok_dev, width), BF16),
        ),
        in_specs=[
            vmem, vmem, pl.BlockSpec(memory_space=pl.ANY), vmem, vmem,
            pl.BlockSpec(memory_space=pltpu.SMEM), vmem, vmem, vmem, vmem, vmem,
        ],
        out_specs=(vmem, vmem),
        scratch_shapes=[
            pltpu.VMEM(pair_band.shape, BF16),
            pltpu.VMEM((GROUP, tok_dev, LANES), BF16),
            pltpu.VMEM((GROUP, tok_dev, 2 * LANES), F32),
            pltpu.VMEM((ext, LANES), BF16),
            pltpu.VMEM((ext, LANES), BF16),
            pltpu.VMEM((atom_dev, LANES), BF16),
            pltpu.VMEM((atom_dev, LANES), F32),
            pltpu.VMEM((atom_dev, group_tok), BF16),
            pltpu.VMEM((blocks, group_tok, LANES), BF16),
            pltpu.VMEM((atom_dev, LANES), jnp.int32),
            pltpu.VMEM((blocks + 2, LANES), jnp.int32),
            pltpu.VMEM((n_pair, 32, LANES), BF16),
            pltpu.VMEM((n_pair * LANES, 4 * LANES), BF16),
            pltpu.VMEM((GROUP, tok_dev, 2 * LANES), BF16),
            pltpu.VMEM((GROUP, tok_dev, 2 * LANES), BF16),
            pltpu.VMEM((n_pair, atom_dev // 4, LANES), BF16),
            pltpu.VMEM((atom_dev, LANES), BF16),
            pltpu.VMEM((GROUP, tok_dev, width), F32),
            pltpu.VMEM((GROUP, tok_dev, width), BF16),
            pltpu.VMEM((GROUP, tok_dev, width), BF16),
            dma((CHUNKS,)),
            dma((GROUP,)), dma((GROUP,)),
            dma((n_pair,)), dma((n_pair,)),
            dma((CHUNKS, GROUP)), dma((CHUNKS, GROUP)),
            dma((2,)), dma((2,)),
            dma((blocks, n_pair)), dma((blocks, n_pair)),
            dma((GROUP,)), dma((GROUP,)),
        ],
        compiler_params=pltpu.CompilerParams(
            collective_id=0, has_side_effects=True, vmem_limit_bytes=48 * 1024 * 1024
        ),
        name="encoder",
    )(
        trunk_single,
        atom_feature,
        pair_band,
        atom_token.reshape(total_atoms // LANES, LANES),
        token_counts.reshape(1, tok_dev),
        key_offsets,
        single_weight,
        attn_weight.reshape(attn_weight.shape[0], attn_weight.shape[2]),
        bias_weight.reshape(1, bias_weight.shape[0]),
        out_weight,
        token_weight,
    )


def solution(mesh):
    placed = (
        P("atoms", None),
        P("atoms", None),
        P("atoms", None, None),
        P(),
        P("atoms"),
        P("atoms"),
        P(),
        P(None, "pair", None),
        P(None, "pair"),
        P("pair", None),
        P(),
    )
    return jax.shard_map(
        shards,
        mesh=mesh,
        in_specs=placed,
        out_specs=(P("atoms", None), P("atoms", None)),
        check_vma=False,
    )
```

time: 432 us -> 47.2 us (0.11)
  the two profiles are of different devices: /device:TPU:24 before, /device:TPU:1 now
where the time goes in v1:
time: 47.2 us; the launch traced here: 46.8 us
  Pallas kernels  36.9 us (78%)
  local copies, waits for them, and re-layouts  9.24 us (20%)
  between operations  0.66 us (1%)
    pallas_call x1, Pallas kernels, shards(): pl.pallas_call(functools.partial(kernel, (n_dev, n_pair, total_atoms)), o...  36.9 us
    unnamed x22, local copies, waits for them, and re-layouts  9.24 us

profile of v1, /device:TPU:1, one launch (start us, length us, event | category | flops | bytes accessed | tf_op | source)
XLA Modules:
  0.0 46.8 jit_solution(14092834520245225069)
XLA Ops:
  0.6 0.0 copy-start
  0.6 0.9 %copy-done = bf16[768,128]{1,0:T(8,128)(2,1)S(1)} copy-done((bf16[768,128]{1,0:T(8,128)(2,1)S(1)}, bf16[768,128]{1,0:T(8,128)(2,1)}, u32[]{:S(2)}) %copy-start) | copy-done | bytes 196632
  1.6 0.0 copy-start.1
  1.6 0.9 %copy-done.1 = s32[49152]{0:T(1024)S(1)} copy-done((s32[49152]{0:T(1024)S(1)}, s32[49152]{0:T(1024)}, u32[]{:S(2)}) %copy-start.1) | copy-done | bytes 196632
  2.5 0.0 copy-start.2
  2.5 0.9 %copy-done.2 = bf16[384,128]{1,0:T(8,128)(2,1)S(1)} copy-done((bf16[384,128]{1,0:T(8,128)(2,1)S(1)}, bf16[384,128]{1,0:T(8,128)(2,1)}, u32[]{:S(2)}) %copy-start.2) | copy-done | bytes 98328
  3.4 0.0 copy-start.3
  3.4 0.9 %copy-done.3 = bf16[128,384]{1,0:T(8,128)(2,1)S(1)} copy-done((bf16[128,384]{1,0:T(8,128)(2,1)S(1)}, bf16[128,384]{1,0:T(8,128)(2,1)}, u32[]{:S(2)}) %copy-start.3) | copy-done | bytes 98328
  4.3 0.0 copy-start.4
  4.3 0.9 %copy-done.4 = bf16[96,384]{1,0:T(8,128)(2,1)S(1)} copy-done((bf16[96,384]{1,0:T(8,128)(2,1)S(1)}, bf16[96,384]{1,0:T(8,128)(2,1)}, u32[]{:S(2)}) %copy-start.4) | copy-done | bytes 73752
  5.2 0.0 copy-start.5
  5.2 0.8 %copy-done.5 = bf16[128,1,128]{2,0,1:T(8,128)(2,1)S(1)} copy-done((bf16[128,1,128]{2,0,1:T(8,128)(2,1)S(1)}, bf16[128,1,128]{2,0,1:T(8,128)(2,1)}, u32[]{:S(2)}) %copy-start.5) | copy-done | bytes 32792
  5.9 0.0 copy-start.6
  5.9 0.7 %copy-done.6 = bf16[32,128]{1,0:T(8,128)(2,1)S(1)} copy-done((bf16[32,128]{1,0:T(8,128)(2,1)S(1)}, bf16[32,128]{1,0:T(8,128)(2,1)}, u32[]{:S(2)}) %copy-start.6) | copy-done | bytes 8216
  6.6 0.0 copy-start.7
  6.6 0.7 %copy-done.7 = s32[96]{0:T(128)S(1)} copy-done((s32[96]{0:T(128)S(1)}, s32[96]{0:T(128)}, u32[]{:S(2)}) %copy-start.7) | copy-done | bytes 408
  7.3 0.0 copy-start.8
  7.3 0.7 %copy-done.8 = s32[24]{0:T(128)S(1)} copy-done((s32[24]{0:T(128)S(1)}, s32[24]{0:T(128)}, u32[]{:S(2)}) %copy-start.8) | copy-done | bytes 120
  7.9 0.0 copy-start.9
  7.9 0.7 %copy-done.9 = f32[128,1]{0,1:T(1,128)S(1)} copy-done((f32[128,1]{0,1:T(1,128)S(1)}, f32[128,1]{0,1:T(1,128)}, u32[]{:S(2)}) %copy-start.9) | copy-done | bytes 536
  8.6 36.9 %encoder.1 = (bf16[768,128]{1,0:T(8,128)(2,1)S(1)}, bf16[96,384]{1,0:T(8,128)(2,1)S(1)}) custom-call(bf16[96,384]{1,0:T(8,128)(2,1)S(1)} %copy-done.4, bf16[768,128]{1,0:T(8,128)(2,1)S(1)} %copy-done, bf16[96,256,128]{2,1,0:T(8,128)(2,1)} %band.1, s32[384,128]{1,0:T(8,128)S(1)} %bitcast.4, s32[1,96]{1,0:T(1,128)S(1)} %bitcast.6, s32[24]{0:T(128)S(1)} %copy-done.8, ...), custom_call_target="tpu_custom_call" | custom-call | tf_op jit(solution)/shard_map/encoder/pallas_call | solution.py:392
  45.5 0.7 %copy.15 = bf16[768,128]{1,0:T(8,128)(2,1)} copy(bf16[768,128]{1,0:T(8,128)(2,1)S(1)} %get-tuple-element.4) | data formatting | bytes 393216
  46.2 0.6 %copy.16 = bf16[96,384]{1,0:T(8,128)(2,1)} copy(bf16[96,384]{1,0:T(8,128)(2,1)S(1)} %get-tuple-element.5) | data formatting | bytes 147456
Async XLA Ops:
  0.6 0.9 %copy-start = (bf16[768,128]{1,0:T(8,128)(2,1)S(1)}, bf16[768,128]{1,0:T(8,128)(2,1)}, u32[]{:S(2)}) copy-start(bf16[768,128]{1,0:T(8,128)(2,1)} %feat.1) | copy-start | bytes 589828
  1.6 0.9 %copy-start.1 = (s32[49152]{0:T(1024)S(1)}, s32[49152]{0:T(1024)}, u32[]{:S(2)}) copy-start(s32[49152]{0:T(1024)} %param.14) | copy-start | bytes 589828
  2.5 0.9 %copy-start.2 = (bf16[384,128]{1,0:T(8,128)(2,1)S(1)}, bf16[384,128]{1,0:T(8,128)(2,1)}, u32[]{:S(2)}) copy-start(bf16[384,128]{1,0:T(8,128)(2,1)} %single_w.1) | copy-start | bytes 294916
  3.4 0.9 %copy-start.3 = (bf16[128,384]{1,0:T(8,128)(2,1)S(1)}, bf16[128,384]{1,0:T(8,128)(2,1)}, u32[]{:S(2)}) copy-start(bf16[128,384]{1,0:T(8,128)(2,1)} %token_w.1) | copy-start | bytes 294916
  4.3 0.9 %copy-start.4 = (bf16[96,384]{1,0:T(8,128)(2,1)S(1)}, bf16[96,384]{1,0:T(8,128)(2,1)}, u32[]{:S(2)}) copy-start(bf16[96,384]{1,0:T(8,128)(2,1)} %trunk.1) | copy-start | bytes 221188
  5.2 0.8 %copy-start.5 = (bf16[128,1,128]{2,0,1:T(8,128)(2,1)S(1)}, bf16[128,1,128]{2,0,1:T(8,128)(2,1)}, u32[]{:S(2)}) copy-start(bf16[128,1,128]{2,0,1:T(8,128)(2,1)} %param.18) | copy-start | bytes 98308
  5.9 0.7 %copy-start.6 = (bf16[32,128]{1,0:T(8,128)(2,1)S(1)}, bf16[32,128]{1,0:T(8,128)(2,1)}, u32[]{:S(2)}) copy-start(bf16[32,128]{1,0:T(8,128)(2,1)} %out_w.1) | copy-start | bytes 24580
  6.6 0.7 %copy-start.7 = (s32[96]{0:T(128)S(1)}, s32[96]{0:T(128)}, u32[]{:S(2)}) copy-start(s32[96]{0:T(128)} %param.15) | copy-start | bytes 1156
  7.3 0.7 %copy-start.8 = (s32[24]{0:T(128)S(1)}, s32[24]{0:T(128)}, u32[]{:S(2)}) copy-start(s32[24]{0:T(128)} %koff.1) | copy-start | bytes 292
  7.9 0.7 %copy-start.9 = (f32[128,1]{0,1:T(1,128)S(1)}, f32[128,1]{0,1:T(1,128)}, u32[]{:S(2)}) copy-start(f32[128,1]{0,1:T(1,128)} %param.19) | copy-start | bytes 1540

commit v2 on v1

--- a/solution.py
+++ b/solution.py
@@ -14,6 +14,7 @@
 F32 = jnp.float32
 BF16 = jnp.bfloat16
 CHUNKS = 4
+UA, UB, UC = 24, 6, 6
 NT = (((1,), (1,)), ((), ()))
 
 
@@ -29,9 +30,11 @@
 
 def kernel(
     sizes,
-    trunk, feat, band, tok, counts, koff, single_w, attn_w, bias_w, out_w, token_w,
+    trunk_h, feat_h, band, tok_h, counts_h, koff_h, single_h, attn_h, bias_h, out_h, token_h,
     atom_out, token_out,
-    band_v, tp_all, bias_all, cond, proj, qs, gate, onehot, onehot_t, tokq, tokl,
+    trunk, feat, tok, counts, koff, single_w, attn_w, bias_w, token_w, in_sem,
+    band_v, tp_all, bias_all, cond, keys, queries, gate, onehot, onehot_t, tok_info, tokl, mine,
+    scores, weights, window_keys,
     ow_all, ow_cat, bias_hi, bias_lo, packed, atoms_bf, sums, sums_out, sums_in,
     band_sem, tp_send, tp_recv, ow_send, ow_recv, bias_send, bias_recv,
     halo_send, halo_recv, gate_send, gate_recv, sum_send, sum_recv,
@@ -69,7 +72,21 @@
         rows = pl.ds(c * part, part)
         return pltpu.make_async_copy(band.at[rows], band_v.at[rows], band_sem.at[c])
 
-    for c in range(CHUNKS):
+    loads = [
+        pltpu.make_async_copy(src, dst, in_sem.at[i])
+        for i, (src, dst) in enumerate(
+            (
+                (trunk_h, trunk), (single_h, single_w), (out_h, ow_all.at[p]), (bias_h, bias_w), (tok_h, tok),
+                (feat_h, feat), (attn_h, attn_w), (koff_h, koff), (token_h, token_w), (counts_h, counts),
+            )
+        )
+    ]
+    for load in loads[:4]:
+        load.start()
+    band_copy(0).start()
+    for load in loads[4:]:
+        load.start()
+    for c in range(1, CHUNKS):
         band_copy(c).start()
 
     def remote(src, dst, send, recv, device):
@@ -135,18 +152,16 @@
         t = lax.rem(r + d, GROUP)
         return remote(sums_out.at[t], sums_in.at[d], sum_send.at[d], sum_recv.at[d], group_peer(d))
 
+    for load in loads[:3]:
+        load.wait()
     tp_all[r] = dot(norm_rows(trunk[...].astype(F32)).astype(BF16), single_w[...]).astype(BF16)
-    ow_all[p] = out_w[...]
-    for i in range(blocks + 2):
-        row = lax.rem(a * blocks + i - 1 + total_atoms // LANES, total_atoms // LANES)
-        tokl[i : i + 1, :] = tok[pl.ds(row, 1), :]
-
     pl.semaphore_wait(barrier, 3 + n_pair - 1 + 2)
     for d in range(1, GROUP):
         tp_copy(d).start()
     for d in range(1, n_pair):
         ow_copy(d).start()
 
+    loads[3].wait()
     w = bias_w[...]
     w_hi = w.astype(BF16).astype(F32)
     w_mid = (w - w_hi).astype(BF16).astype(F32)
@@ -186,28 +201,40 @@
             band_step(c * part + i * 8)
             return inner
 
-        lax.fori_loop(0, part // 8, step, 0)
+        lax.fori_loop(0, part // 8, step, 0, unroll=True)
         for d in range(1, GROUP):
             bias_copy(c, d).start()
         return carry
 
     lax.fori_loop(0, CHUNKS // 2, band_chunk, 0)
 
+    for load in loads[4:]:
+        load.wait()
+    for i in range(blocks + 2):
+        row = lax.rem(a * blocks + i - 1 + total_atoms // LANES, total_atoms // LANES)
+        tokl[i : i + 1, :] = tok[pl.ds(row, 1), :]
     token_base = (base * tok_dev).astype(jnp.int32)
     for d in range(1, GROUP):
         tp_arrive(d).wait_recv()
     cond[0 : first - reach, :] = jnp.zeros((first - reach, LANES), BF16)
     cond[last + reach : last + LANES, :] = jnp.zeros((LANES - reach, LANES), BF16)
 
+    lane1 = lax.broadcasted_iota(jnp.int32, (LANES, LANES), 1)
+
+    def info_block(i, carry):
+        tok_row = tokl[pl.ds(i, 1), :] - token_base
+        spread_row = jnp.broadcast_to(tok_row, (LANES, LANES))
+        tok_info[i] = spread_row.astype(F32).T.astype(jnp.int32)
+        return carry
+
+    lax.fori_loop(0, blocks + 2, info_block, 0, unroll=True)
+
     def cond_block(b, carry):
         rows = pl.ds(pl.multiple_of(b * LANES, LANES), LANES)
         tok_row = tokl[pl.ds(b + 1, 1), :] - token_base
-        spread_row = jnp.broadcast_to(tok_row, (LANES, LANES))
-        tok_col = spread_row.astype(F32).T.astype(jnp.int32)
-        tokq[rows, :] = tok_col + token_base
-        lane = lax.broadcasted_iota(jnp.int32, (LANES, LANES), 1)
+        tok_col = tok_info[b + 1]
         pick = jnp.concatenate(
-            [(tok_col == lane + k * LANES).astype(F32).astype(BF16) for k in range(group_tok // LANES)], axis=1
+            [(tok_col == lane1 + k * LANES).astype(F32).astype(BF16) for k in range(group_tok // LANES)], axis=1
         )
         onehot[rows, :] = pick
         sub = lax.broadcasted_iota(jnp.int32, (group_tok, LANES), 0)
@@ -218,34 +245,62 @@
         ).astype(BF16)
         return carry
 
-    lax.fori_loop(0, blocks, cond_block, 0)
+    lax.fori_loop(0, blocks, cond_block, 0, unroll=True)
     to_right().start()
     to_left().start()
 
     lax.fori_loop(CHUNKS // 2, CHUNKS, band_chunk, 0)
 
-    lane1 = lax.broadcasted_iota(jnp.int32, (LANES, LANES), 1)
     aw = attn_w[...]
     aw32 = aw.astype(F32)
     head = lane1 // 32
     q_w = jnp.where(head == 1, pltpu.roll(aw32, 32, 1), 0.0).astype(BF16)
     g_w = jnp.where(head == 2, pltpu.roll(aw32, LANES - 32, 1), 0.0).astype(BF16)
+    kv_lane = (head == 1) | (head == 2)
+
+    def key_rows(i, normed):
+        place = lax.broadcasted_iota(jnp.int32, (LANES, LANES), 0) + (a * atom_dev + (i - 1) * LANES)
+        absent = jnp.where((place >= 0) & (place < total_atoms), 0.0, -1e30)
+        token = tok_info[i] + LANES
+        info = jnp.where(
+            lane1 == 0,
+            (token >> 4).astype(F32),
+            jnp.where(lane1 == 1, (token & 15).astype(F32), jnp.where(lane1 == 3, absent, jnp.where((lane1 == 2) | (lane1 == 4), 1.0, 0.0))),
+        )
+        keys[pl.ds(pl.multiple_of(i * LANES, LANES), LANES), :] = jnp.where(
+            kv_lane, dot(normed, aw).astype(BF16).astype(F32), info
+        )
 
     def proj_block(b, carry):
         rows = pl.ds(pl.multiple_of(b * LANES, LANES), LANES)
-        ext = pl.ds(pl.multiple_of(first + b * LANES, LANES), LANES)
-        normed = norm_rows(cond[ext, :].astype(F32)).astype(BF16)
-        proj[ext, :] = dot(normed, aw).astype(BF16)
-        qs[rows, :] = dot(normed, q_w).astype(BF16)
+        normed = norm_rows(cond[pl.ds(pl.multiple_of(first + b * LANES, LANES), LANES), :].astype(F32)).astype(BF16)
+        key_rows(b + 1, normed)
+        query = jnp.where(lane1 == 3, 1.0, dot(normed, q_w)).astype(BF16)
+        token = tok_info[b + 1] + LANES
+        against = jnp.where(
+            lane1 == 0,
+            16.0,
+            jnp.where(
+                lane1 == 1,
+                1.0,
+                jnp.where(
+                    lane1 == 2,
+                    (LANES - (token >> 4) * 16).astype(F32),
+                    jnp.where(lane1 == 4, (-(token & 15)).astype(F32), 0.0),
+                ),
+            ),
+        ).astype(BF16)
+        for j in range(4):
+            queries[4 * b + j, 0:32, :] = query[32 * j : 32 * j + 32]
+            queries[4 * b + j, 32:64, :] = against[32 * j : 32 * j + 32]
         gate[rows, :] = jax.nn.sigmoid(dot(normed, g_w).astype(BF16).astype(F32))
         return carry
 
-    lax.fori_loop(0, blocks, proj_block, 0)
+    lax.fori_loop(0, blocks, proj_block, 0, unroll=True)
     to_right().wait_recv()
     to_left().wait_recv()
-    for start in (0, last):
-        normed = norm_rows(cond[start : start + LANES, :].astype(F32)).astype(BF16)
-        proj[start : start + LANES, :] = dot(normed, aw).astype(BF16)
+    for i in (0, blocks + 1):
+        key_rows(i, norm_rows(cond[i * LANES : (i + 1) * LANES, :].astype(F32)).astype(BF16))
 
     for d in range(1, n_pair):
         ow_arrive(d).wait_recv()
@@ -266,53 +321,51 @@
         bias_hi[s] = high
         bias_lo[s] = (whole - high.astype(F32)).astype(BF16)
 
-    width = 3 * LANES
+    mine[...] = dot(onehot[...], bias_hi[...].reshape(group_tok, 2 * LANES)) + dot(
+        onehot[...], bias_lo[...].reshape(group_tok, 2 * LANES)
+    )
+
+    lane32 = lax.broadcasted_iota(jnp.int32, (query_count, LANES), 1) // 32
+    windows = atom_dev // query_count
+
+    def score(w, carry):
+        start = LANES + query_count * w + koff[w]
+        window = keys[pl.ds(start, LANES), :].astype(BF16)
+        window_keys[w] = window
+        scores[w] = lax.dot_general(queries[w], window, NT, preferred_element_type=F32)
+        return carry
+
+    lax.fori_loop(0, windows, score, 0, unroll=UA)
+
+    def soften(b, carry):
+        rows = pl.ds(pl.multiple_of(b * LANES, LANES), LANES)
+        raw = scores[pl.ds(4 * b, 4)]
+        index = raw[:, query_count:].reshape(LANES, LANES).astype(jnp.int32)
+        wrapped = index & (LANES - 1)
+        low = jnp.take_along_axis(mine[rows, :LANES], wrapped, axis=1, mode="promise_in_bounds")
+        high = jnp.take_along_axis(mine[rows, LANES:], wrapped, axis=1, mode="promise_in_bounds")
+        value = raw[:, :query_count].reshape(LANES, LANES) * (1.0 / math.sqrt(32.0)) + jnp.where(
+            index >= LANES, high, low
+        )
+        exponent = jnp.exp(value - jnp.max(value, axis=1, keepdims=True))
+        weights[rows, :] = (exponent * (1.0 / jnp.sum(exponent, axis=1, keepdims=True))).astype(BF16)
+        return carry
+
+    lax.fori_loop(0, blocks, soften, 0, unroll=UB)
 
     def attend(b, carry):
-        rows = pl.ds(pl.multiple_of(b * LANES, LANES), LANES)
-        keys = proj[pl.ds(pl.multiple_of(b * LANES, LANES), width), :]
-        raw = lax.dot_general(qs[rows, :], keys, NT, preferred_element_type=F32) * (1.0 / math.sqrt(32.0))
-        pick = onehot[rows, :]
-        mine = dot(pick, bias_hi[...].reshape(group_tok, 2 * LANES)) + dot(
-            pick, bias_lo[...].reshape(group_tok, 2 * LANES)
-        )
-        low, high = mine[:, :LANES], mine[:, LANES:]
-        my_tok = tokq[rows, :]
-        sub = lax.broadcasted_iota(jnp.int32, (LANES, LANES), 0)
-        window = sub // query_count
-        offset = jnp.where(
-            window == 0,
-            koff[4 * b],
-            jnp.where(window == 1, koff[4 * b + 1], jnp.where(window == 2, koff[4 * b + 2], koff[4 * b + 3])),
-        )
-        shift = offset + window * query_count
-        pieces = []
-        for t in range(3):
-            index = tokl[pl.ds(b + t, 1), :] - my_tok + LANES
-            wrapped = index & (LANES - 1)
-            first_half = jnp.take_along_axis(low, wrapped, axis=1, mode="promise_in_bounds")
-            second_half = jnp.take_along_axis(high, wrapped, axis=1, mode="promise_in_bounds")
-            value = raw[:, t * LANES : (t + 1) * LANES] + jnp.where(index >= LANES, second_half, first_half)
-            slot = lane1 + (t - 1) * LANES - shift
-            place = lane1 + (a * atom_dev + (b + t - 1) * LANES)
-            valid = (slot >= 0) & (slot < LANES) & (place >= 0) & (place < total_atoms)
-            pieces.append(jnp.where(valid, value, -jnp.inf))
-        masked = jnp.concatenate(pieces, axis=1)
-        top = jnp.max(masked, axis=1, keepdims=True)
-        exponent = jnp.exp(masked - top)
-        weights = (exponent / jnp.sum(exponent, axis=1, keepdims=True)).astype(BF16)
-        gated = gate[rows, :] * dot(weights, keys)
-        lane32 = lax.broadcasted_iota(jnp.int32, (query_count, LANES), 1) // 32
         out = jnp.zeros((query_count, LANES), F32)
         for j in range(4):
-            turned = pltpu.roll(gated[32 * j : 32 * j + 32], (32 * j + 64) % LANES, 1)
+            rows = pl.ds(pl.multiple_of(b * LANES + query_count * j, 32), query_count)
+            gated = gate[rows, :] * dot(weights[rows, :], window_keys[4 * b + j])
+            turned = gated if j == 2 else pltpu.roll(gated, (32 * j + 64) % LANES, 1)
             out = jnp.where(lane32 == j, turned, out)
         packed[p, pl.ds(pl.multiple_of(b * query_count, 32), query_count), :] = out.astype(BF16)
-        for d in range(1, n_pair):
+        for d in (2, 1, 3):
             gate_copy(b, d).start()
         return carry
 
-    lax.fori_loop(0, blocks, attend, 0)
+    lax.fori_loop(0, blocks, attend, 0, unroll=UC)
 
     def wait_gate(b, carry):
         for d in range(1, n_pair):
@@ -396,22 +449,36 @@
             jax.ShapeDtypeStruct((tok_dev, width), BF16),
         ),
         in_specs=[
-            vmem, vmem, pl.BlockSpec(memory_space=pl.ANY), vmem, vmem,
-            pl.BlockSpec(memory_space=pltpu.SMEM), vmem, vmem, vmem, vmem, vmem,
-        ],
+            pl.BlockSpec(memory_space=pl.ANY),
+        ]
+        * 11,
         out_specs=(vmem, vmem),
         scratch_shapes=[
+            pltpu.VMEM(trunk_single.shape, BF16),
+            pltpu.VMEM(atom_feature.shape, BF16),
+            pltpu.VMEM((total_atoms // LANES, LANES), jnp.int32),
+            pltpu.VMEM((1, tok_dev), jnp.int32),
+            pltpu.SMEM(key_offsets.shape, jnp.int32),
+            pltpu.VMEM(single_weight.shape, BF16),
+            pltpu.VMEM((LANES, LANES), BF16),
+            pltpu.VMEM((1, LANES), F32),
+            pltpu.VMEM(token_weight.shape, BF16),
+            dma((10,)),
             pltpu.VMEM(pair_band.shape, BF16),
             pltpu.VMEM((GROUP, tok_dev, LANES), BF16),
             pltpu.VMEM((GROUP, tok_dev, 2 * LANES), F32),
             pltpu.VMEM((ext, LANES), BF16),
-            pltpu.VMEM((ext, LANES), BF16),
-            pltpu.VMEM((atom_dev, LANES), BF16),
+            pltpu.VMEM((ext, LANES), F32),
+            pltpu.VMEM((atom_dev // 32, 64, LANES), BF16),
             pltpu.VMEM((atom_dev, LANES), F32),
             pltpu.VMEM((atom_dev, group_tok), BF16),
             pltpu.VMEM((blocks, group_tok, LANES), BF16),
-            pltpu.VMEM((atom_dev, LANES), jnp.int32),
+            pltpu.VMEM((blocks + 2, LANES, LANES), jnp.int32),
             pltpu.VMEM((blocks + 2, LANES), jnp.int32),
+            pltpu.VMEM((atom_dev, 2 * LANES), F32),
+            pltpu.VMEM((atom_dev // 32, 64, LANES), F32),
+            pltpu.VMEM((atom_dev, LANES), BF16),
+            pltpu.VMEM((atom_dev // 32, LANES, LANES), BF16),
             pltpu.VMEM((n_pair, 32, LANES), BF16),
             pltpu.VMEM((n_pair * LANES, 4 * LANES), BF16),
             pltpu.VMEM((GROUP, tok_dev, 2 * LANES), BF16),
@@ -434,17 +501,22 @@
         ),
         name="encoder",
     )(
-        trunk_single,
-        atom_feature,
-        pair_band,
-        atom_token.reshape(total_atoms // LANES, LANES),
-        token_counts.reshape(1, tok_dev),
-        key_offsets,
-        single_weight,
-        attn_weight.reshape(attn_weight.shape[0], attn_weight.shape[2]),
-        bias_weight.reshape(1, bias_weight.shape[0]),
-        out_weight,
-        token_weight,
+        *(
+            pltpu.with_memory_space_constraint(value, pltpu.HBM)
+            for value in (
+                trunk_single,
+                atom_feature,
+                pair_band,
+                atom_token.reshape(total_atoms // LANES, LANES),
+                token_counts.reshape(1, tok_dev),
+                key_offsets,
+                single_weight,
+                attn_weight.reshape(attn_weight.shape[0], attn_weight.shape[2]),
+                bias_weight.reshape(1, bias_weight.shape[0]),
+                out_weight,
+                token_weight,
+            )
+        )
     )
 
 

time: 47.2 us -> 35 us (0.74)
  local copies, waits for them, and re-layouts: 9.24 us -> 1.31 us
  Pallas kernels: 36.9 us -> 32.9 us
    unnamed x22 -> x2, local copies, waits for them, and re-layouts: 9.24 us -> 1.31 us
    pallas_call x1, Pallas kernels: 36.9 us -> 32.9 us  [shards(): pl.pallas_call(functools.partial(kernel, (n_dev, n_pair, total_atoms)), o...]
where the time goes in v2:
time: 35 us; the launch traced here: 34.9 us
  Pallas kernels  32.9 us (94%)
  local copies, waits for them, and re-layouts  1.31 us (4%)
  between operations  0.64 us (2%)
    pallas_call x1, Pallas kernels, shards(): pl.pallas_call(functools.partial(kernel, (n_dev, n_pair, total_atoms)), o...  32.9 us
    unnamed x2, local copies, waits for them, and re-layouts  1.31 us

profile of v2, /device:TPU:1, one launch (start us, length us, event | category | flops | bytes accessed | tf_op | source)
XLA Modules:
  0.0 34.9 jit_solution(2697864401074082272)
XLA Ops:
  0.6 32.9 %encoder.1 = (bf16[768,128]{1,0:T(8,128)(2,1)S(1)}, bf16[96,384]{1,0:T(8,128)(2,1)S(1)}) custom-call(bf16[96,384]{1,0:T(8,128)(2,1)} %trunk_h.1, bf16[768,128]{1,0:T(8,128)(2,1)} %feat_h.1, bf16[96,256,128]{2,1,0:T(8,128)(2,1)} %band.1, s32[384,128]{1,0:T(8,128)} %bitcast.4, s32[1,96]{1,0:T(1,128)} %bitcast.6, s32[24]{0:T(128)} %koff_h.1, ...), custom_call_target="tpu_custom_call" | custom-call | tf_op jit(solution)/shard_map/encoder/pallas_call | solution.py:445
  33.6 0.7 %copy.15 = bf16[768,128]{1,0:T(8,128)(2,1)} copy(bf16[768,128]{1,0:T(8,128)(2,1)S(1)} %get-tuple-element.4) | data formatting | bytes 393216
  34.2 0.6 %copy.16 = bf16[96,384]{1,0:T(8,128)(2,1)} copy(bf16[96,384]{1,0:T(8,128)(2,1)S(1)} %get-tuple-element.5) | data formatting | bytes 147456

commit v3 on v2

--- a/solution.py
+++ b/solution.py
@@ -14,7 +14,8 @@
 F32 = jnp.float32
 BF16 = jnp.bfloat16
 CHUNKS = 4
-UA, UB, UC = 24, 6, 6
+SEND = 3
+PARTS = ((0, 6),)
 NT = (((1,), (1,)), ((), ()))
 
 
@@ -41,7 +42,7 @@
 ):
     n_dev, n_pair, total_atoms = sizes
     tok_dev = trunk.shape[0]
-    atom_dev = feat.shape[0]
+    atom_dev = feat_h.shape[0]
     blocks = atom_dev // LANES
     reach = 96
     query_count = 32
@@ -77,7 +78,7 @@
         for i, (src, dst) in enumerate(
             (
                 (trunk_h, trunk), (single_h, single_w), (out_h, ow_all.at[p]), (bias_h, bias_w), (tok_h, tok),
-                (feat_h, feat), (attn_h, attn_w), (koff_h, koff), (token_h, token_w), (counts_h, counts),
+                (feat_h, feat.at[pl.ds(LANES, atom_dev)]), (attn_h, attn_w), (koff_h, koff), (token_h, token_w), (counts_h, counts),
             )
         )
     ]
@@ -94,12 +95,34 @@
             src_ref=src, dst_ref=dst, send_sem=send, recv_sem=recv, device_id=device, device_id_type=MESH
         )
 
+    def sends(d, act):
+        if d == 2:
+            act()
+        else:
+            pl.when(r != (GROUP - 1 if d == 1 else 0))(act)
+
+    def receives(d, act):
+        if d == 2:
+            act()
+        else:
+            pl.when(r != (0 if d == 1 else GROUP - 1))(act)
+
+    def tp_rows(s):
+        return tp_all.at[pl.ds(pl.multiple_of(s * tok_dev, 16), tok_dev)]
+
     def tp_copy(d):
-        return remote(tp_all.at[r], tp_all.at[r], tp_send.at[d], tp_recv.at[d], group_peer(d))
+        return remote(tp_rows(r), tp_rows(r), tp_send.at[d], tp_recv.at[d], group_peer(d))
 
     def tp_arrive(d):
         s = lax.rem(r + GROUP - d, GROUP)
-        return remote(tp_all.at[s], tp_all.at[s], tp_send.at[d], tp_recv.at[d], group_peer(d))
+        return remote(tp_rows(s), tp_rows(s), tp_send.at[d], tp_recv.at[d], group_peer(d))
+
+    def tp_outside(neighbour):
+        return remote(tp_rows(r), tp_rows(GROUP), tp_send.at[0], tp_recv.at[0], (neighbour, p))
+
+    def outside(act):
+        pl.when(r == 0)(lambda: act(tp_outside(left)))
+        pl.when(r == GROUP - 1)(lambda: act(tp_outside(right)))
 
     def ow_copy(d):
         return remote(ow_all.at[p], ow_all.at[p], ow_send.at[d], ow_recv.at[d], pair_peer(d))
@@ -125,42 +148,36 @@
 
     def to_right():
         return remote(
-            cond.at[pl.ds(last - reach, reach)], cond.at[pl.ds(first - reach, reach)],
+            feat_h.at[pl.ds(atom_dev - reach, reach)], feat.at[pl.ds(first - reach, reach)],
             halo_send.at[0], halo_recv.at[0], (right, p),
         )
 
     def to_left():
         return remote(
-            cond.at[pl.ds(first, reach)], cond.at[pl.ds(last, reach)],
+            feat_h.at[pl.ds(0, reach)], feat.at[pl.ds(last, reach)],
             halo_send.at[1], halo_recv.at[1], (left, p),
         )
 
     def gate_copy(b, d):
-        rows = pl.ds(b * query_count, query_count)
+        rows = pl.ds(b * query_count * SEND, query_count * SEND)
         return remote(
             packed.at[p, rows], packed.at[p, rows], gate_send.at[b, d], gate_recv.at[b, d], pair_peer(d)
         )
 
     def gate_arrive(b, d):
         s = lax.rem(p + n_pair - d, n_pair)
-        rows = pl.ds(b * query_count, query_count)
+        rows = pl.ds(b * query_count * SEND, query_count * SEND)
         return remote(
             packed.at[s, rows], packed.at[s, rows], gate_send.at[b, d], gate_recv.at[b, d], pair_peer(d)
         )
 
-    def sum_copy(d):
+    def sum_copy(c, d):
         t = lax.rem(r + d, GROUP)
-        return remote(sums_out.at[t], sums_in.at[d], sum_send.at[d], sum_recv.at[d], group_peer(d))
+        return remote(sums_out.at[t, c], sums_in.at[d, c], sum_send.at[c, d], sum_recv.at[c, d], group_peer(d))
 
     for load in loads[:3]:
         load.wait()
-    tp_all[r] = dot(norm_rows(trunk[...].astype(F32)).astype(BF16), single_w[...]).astype(BF16)
-    pl.semaphore_wait(barrier, 3 + n_pair - 1 + 2)
-    for d in range(1, GROUP):
-        tp_copy(d).start()
-    for d in range(1, n_pair):
-        ow_copy(d).start()
-
+    tp_all[pl.ds(pl.multiple_of(r * tok_dev, 16), tok_dev), :] = dot(norm_rows(trunk[...].astype(F32)).astype(BF16), single_w[...]).astype(BF16)
     loads[3].wait()
     w = bias_w[...]
     w_hi = w.astype(BF16).astype(F32)
@@ -194,62 +211,74 @@
             halves.append((products - mean * w_total) * lax.rsqrt(spread + 1e-05))
         bias_all[r, pl.ds(pl.multiple_of(start, 8), 8), :] = jnp.concatenate(halves, axis=1)
 
-    def band_chunk(c, carry):
+    def band_chunk(c):
         band_copy(c).wait()
-
-        def step(i, inner):
+        for i in range(part // 8):
             band_step(c * part + i * 8)
-            return inner
-
-        lax.fori_loop(0, part // 8, step, 0, unroll=True)
-        for d in range(1, GROUP):
-            bias_copy(c, d).start()
-        return carry
-
-    lax.fori_loop(0, CHUNKS // 2, band_chunk, 0)
-
+
+    def send_bias(c):
+        for d in (2, 1, 3):
+            sends(d, lambda: bias_copy(c, d).start())
+
+    def clear(slot, distance):
+        bias_all[slot] = jnp.zeros(bias_all.shape[1:], F32)
+        sums_in[distance] = jnp.zeros(sums_in.shape[1:], BF16)
+
+    pl.when(r == 0)(lambda: clear(GROUP - 1, 1))
+    pl.when(r == GROUP - 1)(lambda: clear(0, GROUP - 1))
+
+    feat[0 : first - reach, :] = jnp.zeros((first - reach, LANES), BF16)
+    feat[last + reach : last + LANES, :] = jnp.zeros((LANES - reach, LANES), BF16)
+    tp_all[(GROUP + 1) * tok_dev :, :] = jnp.zeros((tp_all.shape[0] - (GROUP + 1) * tok_dev, LANES), BF16)
+
+    @pl.when((r > 0) & (r < GROUP - 1))
+    def no_outside():
+        tp_all[GROUP * tok_dev : (GROUP + 1) * tok_dev, :] = jnp.zeros((tok_dev, LANES), BF16)
+
+    band_chunk(0)
+    pl.semaphore_wait(barrier, 3 + n_pair - 1 + 2)
+    for d in (2, 1, 3):
+        tp_copy(d).start()
+    outside(lambda copy: copy.start())
+    to_right().start()
+    to_left().start()
+    send_bias(0)
+    for d in range(1, n_pair):
+        ow_copy(d).start()
+    for c in range(1, CHUNKS):
+        band_chunk(c)
+        send_bias(c)
+
+    token_base = (base * tok_dev).astype(jnp.int32)
     for load in loads[4:]:
         load.wait()
     for i in range(blocks + 2):
         row = lax.rem(a * blocks + i - 1 + total_atoms // LANES, total_atoms // LANES)
         tokl[i : i + 1, :] = tok[pl.ds(row, 1), :]
-    token_base = (base * tok_dev).astype(jnp.int32)
+    lane1 = lax.broadcasted_iota(jnp.int32, (LANES, LANES), 1)
+    sub = lax.broadcasted_iota(jnp.int32, (group_tok, LANES), 0)
+    for i in range(blocks + 2):
+        tok_row = tokl[i : i + 1, :] - token_base
+        tok_col = jnp.broadcast_to(tok_row, (LANES, LANES)).astype(F32).T.astype(jnp.int32)
+        tok_info[i] = tok_col
+        wanted = jnp.where(tok_col < 0, tok_col + (GROUP + 1) * tok_dev, tok_col)
+        onehot[i * LANES : (i + 1) * LANES, :] = jnp.concatenate(
+            [(wanted == lane1 + k * LANES).astype(F32).astype(BF16) for k in range(onehot.shape[1] // LANES)], axis=1
+        )
+        if 1 <= i <= blocks:
+            onehot_t[:, (i - 1) * LANES : i * LANES] = (
+                (jnp.broadcast_to(tok_row, (group_tok, LANES)) == sub).astype(F32).astype(BF16)
+            )
+
     for d in range(1, GROUP):
         tp_arrive(d).wait_recv()
-    cond[0 : first - reach, :] = jnp.zeros((first - reach, LANES), BF16)
-    cond[last + reach : last + LANES, :] = jnp.zeros((LANES - reach, LANES), BF16)
-
-    lane1 = lax.broadcasted_iota(jnp.int32, (LANES, LANES), 1)
-
-    def info_block(i, carry):
-        tok_row = tokl[pl.ds(i, 1), :] - token_base
-        spread_row = jnp.broadcast_to(tok_row, (LANES, LANES))
-        tok_info[i] = spread_row.astype(F32).T.astype(jnp.int32)
-        return carry
-
-    lax.fori_loop(0, blocks + 2, info_block, 0, unroll=True)
-
-    def cond_block(b, carry):
-        rows = pl.ds(pl.multiple_of(b * LANES, LANES), LANES)
-        tok_row = tokl[pl.ds(b + 1, 1), :] - token_base
-        tok_col = tok_info[b + 1]
-        pick = jnp.concatenate(
-            [(tok_col == lane1 + k * LANES).astype(F32).astype(BF16) for k in range(group_tok // LANES)], axis=1
-        )
-        onehot[rows, :] = pick
-        sub = lax.broadcasted_iota(jnp.int32, (group_tok, LANES), 0)
-        onehot_t[b] = (jnp.broadcast_to(tok_row, (group_tok, LANES)) == sub).astype(F32).astype(BF16)
-        chosen = dot(pick, tp_all[...].reshape(group_tok, LANES)).astype(BF16)
-        cond[pl.ds(pl.multiple_of(first + b * LANES, LANES), LANES), :] = (
-            feat[rows, :].astype(F32) + chosen.astype(F32)
-        ).astype(BF16)
-        return carry
-
-    lax.fori_loop(0, blocks, cond_block, 0, unroll=True)
-    to_right().start()
-    to_left().start()
-
-    lax.fori_loop(CHUNKS // 2, CHUNKS, band_chunk, 0)
+    outside(lambda copy: copy.wait_recv())
+    to_right().wait_recv()
+    to_left().wait_recv()
+    for i in range(blocks + 2):
+        rows = slice(i * LANES, (i + 1) * LANES)
+        chosen = dot(onehot[rows, :], tp_all[...]).astype(BF16)
+        cond[rows, :] = (feat[rows, :].astype(F32) + chosen.astype(F32)).astype(BF16)
 
     aw = attn_w[...]
     aw32 = aw.astype(F32)
@@ -297,8 +326,6 @@
         return carry
 
     lax.fori_loop(0, blocks, proj_block, 0, unroll=True)
-    to_right().wait_recv()
-    to_left().wait_recv()
     for i in (0, blocks + 1):
         key_rows(i, norm_rows(cond[i * LANES : (i + 1) * LANES, :].astype(F32)).astype(BF16))
 
@@ -309,22 +336,6 @@
         for j in range(4):
             ow_cat[h * LANES + 32 * j : h * LANES + 32 * j + 32, j * LANES : (j + 1) * LANES] = ow_all[h]
 
-    def wait_bias(c, carry):
-        for d in range(1, GROUP):
-            bias_arrive(c, d).wait_recv()
-        return carry
-
-    lax.fori_loop(0, CHUNKS, wait_bias, 0)
-    for s in range(GROUP):
-        whole = bias_all[s]
-        high = whole.astype(BF16)
-        bias_hi[s] = high
-        bias_lo[s] = (whole - high.astype(F32)).astype(BF16)
-
-    mine[...] = dot(onehot[...], bias_hi[...].reshape(group_tok, 2 * LANES)) + dot(
-        onehot[...], bias_lo[...].reshape(group_tok, 2 * LANES)
-    )
-
     lane32 = lax.broadcasted_iota(jnp.int32, (query_count, LANES), 1) // 32
     windows = atom_dev // query_count
 
@@ -335,7 +346,23 @@
         scores[w] = lax.dot_general(queries[w], window, NT, preferred_element_type=F32)
         return carry
 
-    lax.fori_loop(0, windows, score, 0, unroll=UA)
+
+    for w in range(windows):
+        score(w, 0)
+
+    for c in range(CHUNKS):
+        for d in range(1, GROUP):
+            receives(d, lambda: bias_arrive(c, d).wait_recv())
+    for s in range(GROUP):
+        whole = bias_all[s]
+        high = whole.astype(BF16)
+        bias_hi[s] = high
+        bias_lo[s] = (whole - high.astype(F32)).astype(BF16)
+
+    both = jnp.concatenate([bias_hi[...].reshape(group_tok, 2 * LANES), bias_lo[...].reshape(group_tok, 2 * LANES)], axis=0)
+    for b in range(blocks):
+        pick = onehot[first + b * LANES : first + (b + 1) * LANES, :group_tok]
+        mine[b * LANES : (b + 1) * LANES, :] = dot(jnp.concatenate([pick, pick], axis=1), both)
 
     def soften(b, carry):
         rows = pl.ds(pl.multiple_of(b * LANES, LANES), LANES)
@@ -351,7 +378,6 @@
         weights[rows, :] = (exponent * (1.0 / jnp.sum(exponent, axis=1, keepdims=True))).astype(BF16)
         return carry
 
-    lax.fori_loop(0, blocks, soften, 0, unroll=UB)
 
     def attend(b, carry):
         out = jnp.zeros((query_count, LANES), F32)
@@ -361,71 +387,74 @@
             turned = gated if j == 2 else pltpu.roll(gated, (32 * j + 64) % LANES, 1)
             out = jnp.where(lane32 == j, turned, out)
         packed[p, pl.ds(pl.multiple_of(b * query_count, 32), query_count), :] = out.astype(BF16)
+        return carry
+
+    for b in range(blocks):
+        soften(b, 0)
+    for b in range(blocks):
+        attend(b, 0)
+
+    for b in range(blocks // SEND):
         for d in (2, 1, 3):
             gate_copy(b, d).start()
-        return carry
-
-    lax.fori_loop(0, blocks, attend, 0, unroll=UC)
-
-    def wait_gate(b, carry):
-        for d in range(1, n_pair):
-            gate_arrive(b, d).wait_recv()
-        return carry
-
-    lax.fori_loop(0, blocks, wait_gate, 0)
-
-    update = dot(packed[0], ow_cat[0:LANES, :])
-    for h in range(1, n_pair):
-        update = update + dot(packed[h], ow_cat[h * LANES : (h + 1) * LANES, :])
-    for b in range(blocks):
-        for j in range(4):
-            at = b * LANES + 32 * j
-            value = cond[first + at : first + at + 32, :].astype(F32) + update[
-                32 * b : 32 * b + 32, j * LANES : (j + 1) * LANES
-            ]
-            atoms_bf[at : at + 32, :] = value.astype(BF16)
-    atom_out[...] = atoms_bf[...]
-    total = None
-    for b in range(blocks):
-        per_atom = jnp.maximum(dot(atoms_bf[b * LANES : (b + 1) * LANES, :], token_w[...]), 0.0).astype(BF16)
-        term = dot(onehot_t[b], per_atom)
-        total = term if total is None else total + term
-    for s in range(GROUP):
-        sums[s] = total[s * tok_dev : (s + 1) * tok_dev]
-        sums_out[s] = total[s * tok_dev : (s + 1) * tok_dev].astype(BF16)
-    for d in range(1, GROUP):
-        sum_copy(d).start()
+
+    column_blocks = sums.shape[1]
+    for k, (begin, end) in enumerate(PARTS):
+        for b in range(blocks // SEND):
+            for d in range(1, n_pair):
+                gate_arrive(b, d).wait_recv()
+        rows = slice(32 * begin, 32 * end)
+        update = dot(packed[0, rows], ow_cat[0:LANES, :])
+        for h in range(1, n_pair):
+            update = update + dot(packed[h, rows], ow_cat[h * LANES : (h + 1) * LANES, :])
+        for b in range(begin, end):
+            for j in range(4):
+                at = b * LANES + 32 * j
+                value = cond[first + at : first + at + 32, :].astype(F32) + update[
+                    32 * (b - begin) : 32 * (b - begin) + 32, j * LANES : (j + 1) * LANES
+                ]
+                atoms_bf[at : at + 32, :] = value.astype(BF16)
+        span = slice(begin * LANES, end * LANES)
+        atom_out[span, :] = atoms_bf[span, :]
+        for c in range(column_blocks):
+            per_atom = jnp.maximum(dot(atoms_bf[span, :], token_w[:, c * LANES : (c + 1) * LANES]), 0.0).astype(BF16)
+            total = dot(onehot_t[:, span], per_atom)
+            for t in range(GROUP):
+                here = total[t * tok_dev : (t + 1) * tok_dev]
+                if k > 0:
+                    here = here + sums[t, c]
+                sums[t, c] = here
+                if k == len(PARTS) - 1:
+                    sums_out[t, c] = here.astype(BF16)
+            if k == len(PARTS) - 1:
+                for d in (2, 1, 3):
+                    sends(d, lambda: sum_copy(c, d).start())
     eye = lax.broadcasted_iota(jnp.int32, (tok_dev, tok_dev), 0) == lax.broadcasted_iota(
         jnp.int32, (tok_dev, tok_dev), 1
     )
     count = jnp.sum(jnp.where(eye, counts[...].astype(F32), 0.0), axis=1, keepdims=True)
-    result = sums[r]
-    for d in range(1, GROUP):
-        sum_copy(d).wait_recv()
-        result = result + sums_in[d].astype(F32)
-    token_out[...] = (result / count).astype(BF16)
+    inverse = 1.0 / count
+    for c in range(column_blocks):
+        for d in range(1, GROUP):
+            receives(d, lambda: sum_copy(c, d).wait_recv())
+        result = sums[r, c]
+        for d in range(1, GROUP):
+            result = result + sums_in[d, c].astype(F32)
+        token_out[:, c * LANES : (c + 1) * LANES] = (result * inverse).astype(BF16)
 
     for d in range(1, GROUP):
         tp_copy(d).wait_send()
-        sum_copy(d).wait_send()
+        for c in range(column_blocks):
+            sends(d, lambda: sum_copy(c, d).wait_send())
+        for c in range(CHUNKS):
+            sends(d, lambda: bias_copy(c, d).wait_send())
     for d in range(1, n_pair):
         ow_copy(d).wait_send()
+        for b in range(blocks // SEND):
+            gate_copy(b, d).wait_send()
+    outside(lambda copy: copy.wait_send())
     to_right().wait_send()
     to_left().wait_send()
-
-    def drain_bias(c, carry):
-        for d in range(1, GROUP):
-            bias_copy(c, d).wait_send()
-        return carry
-
-    lax.fori_loop(0, CHUNKS, drain_bias, 0)
-
-    def drain_gate(b, carry):
-        for d in range(1, n_pair):
-            gate_copy(b, d).wait_send()
-        return carry
-
-    lax.fori_loop(0, blocks, drain_gate, 0)
 
 
 def shards(
@@ -455,7 +484,7 @@
         out_specs=(vmem, vmem),
         scratch_shapes=[
             pltpu.VMEM(trunk_single.shape, BF16),
-            pltpu.VMEM(atom_feature.shape, BF16),
+            pltpu.VMEM((ext, LANES), BF16),
             pltpu.VMEM((total_atoms // LANES, LANES), jnp.int32),
             pltpu.VMEM((1, tok_dev), jnp.int32),
             pltpu.SMEM(key_offsets.shape, jnp.int32),
@@ -465,14 +494,14 @@
             pltpu.VMEM(token_weight.shape, BF16),
             dma((10,)),
             pltpu.VMEM(pair_band.shape, BF16),
-            pltpu.VMEM((GROUP, tok_dev, LANES), BF16),
+            pltpu.VMEM((group_tok + LANES, LANES), BF16),
             pltpu.VMEM((GROUP, tok_dev, 2 * LANES), F32),
             pltpu.VMEM((ext, LANES), BF16),
             pltpu.VMEM((ext, LANES), F32),
             pltpu.VMEM((atom_dev // 32, 64, LANES), BF16),
             pltpu.VMEM((atom_dev, LANES), F32),
-            pltpu.VMEM((atom_dev, group_tok), BF16),
-            pltpu.VMEM((blocks, group_tok, LANES), BF16),
+            pltpu.VMEM((ext, group_tok + LANES), BF16),
+            pltpu.VMEM((group_tok, atom_dev), BF16),
             pltpu.VMEM((blocks + 2, LANES, LANES), jnp.int32),
             pltpu.VMEM((blocks + 2, LANES), jnp.int32),
             pltpu.VMEM((atom_dev, 2 * LANES), F32),
@@ -485,16 +514,16 @@
             pltpu.VMEM((GROUP, tok_dev, 2 * LANES), BF16),
             pltpu.VMEM((n_pair, atom_dev // 4, LANES), BF16),
             pltpu.VMEM((atom_dev, LANES), BF16),
-            pltpu.VMEM((GROUP, tok_dev, width), F32),
-            pltpu.VMEM((GROUP, tok_dev, width), BF16),
-            pltpu.VMEM((GROUP, tok_dev, width), BF16),
+            pltpu.VMEM((GROUP, width // LANES, tok_dev, LANES), F32),
+            pltpu.VMEM((GROUP, width // LANES, tok_dev, LANES), BF16),
+            pltpu.VMEM((GROUP, width // LANES, tok_dev, LANES), BF16),
             dma((CHUNKS,)),
             dma((GROUP,)), dma((GROUP,)),
             dma((n_pair,)), dma((n_pair,)),
             dma((CHUNKS, GROUP)), dma((CHUNKS, GROUP)),
             dma((2,)), dma((2,)),
             dma((blocks, n_pair)), dma((blocks, n_pair)),
-            dma((GROUP,)), dma((GROUP,)),
+            dma((width // LANES, GROUP)), dma((width // LANES, GROUP)),
         ],
         compiler_params=pltpu.CompilerParams(
             collective_id=0, has_side_effects=True, vmem_limit_bytes=48 * 1024 * 1024

time: 35 us -> 30.4 us (0.87)
  Pallas kernels: 32.9 us -> 28.4 us
    pallas_call x1, Pallas kernels: 32.9 us -> 28.4 us  [shards(): pl.pallas_call(functools.partial(kernel, (n_dev, n_pair, total_atoms)), o...]
where the time goes in v3:
time: 30.4 us; the launch traced here: 30.3 us
  Pallas kernels  28.4 us (93%)
  local copies, waits for them, and re-layouts  1.31 us (4%)
  between operations  0.64 us (2%)
    pallas_call x1, Pallas kernels, shards(): pl.pallas_call(functools.partial(kernel, (n_dev, n_pair, total_atoms)), o...  28.4 us
    unnamed x2, local copies, waits for them, and re-layouts  1.31 us

profile of v3, /device:TPU:1, one launch (start us, length us, event | category | flops | bytes accessed | tf_op | source)
XLA Modules:
  0.0 30.3 jit_solution(1867884314052095508)
XLA Ops:
  0.6 28.4 %encoder.1 = (bf16[768,128]{1,0:T(8,128)(2,1)S(1)}, bf16[96,384]{1,0:T(8,128)(2,1)S(1)}) custom-call(bf16[96,384]{1,0:T(8,128)(2,1)} %trunk_h.1, bf16[768,128]{1,0:T(8,128)(2,1)} %feat_h.1, bf16[96,256,128]{2,1,0:T(8,128)(2,1)} %band.1, s32[384,128]{1,0:T(8,128)} %bitcast.4, s32[1,96]{1,0:T(1,128)} %bitcast.6, s32[24]{0:T(128)} %koff_h.1, ...), custom_call_target="tpu_custom_call" | custom-call | tf_op jit(solution)/shard_map/encoder/pallas_call | solution.py:474
  29.0 0.7 %copy.15 = bf16[768,128]{1,0:T(8,128)(2,1)} copy(bf16[768,128]{1,0:T(8,128)(2,1)S(1)} %get-tuple-element.4) | data formatting | bytes 393216
  29.7 0.6 %copy.16 = bf16[96,384]{1,0:T(8,128)(2,1)} copy(bf16[96,384]{1,0:T(8,128)(2,1)S(1)} %get-tuple-element.5) | data formatting | bytes 147456

commit v4 on v3

--- a/solution.py
+++ b/solution.py
@@ -14,7 +14,7 @@
 F32 = jnp.float32
 BF16 = jnp.bfloat16
 CHUNKS = 4
-SEND = 3
+SEND = 6
 PARTS = ((0, 6),)
 NT = (((1,), (1,)), ((), ()))
 
@@ -173,10 +173,15 @@
 
     def sum_copy(c, d):
         t = lax.rem(r + d, GROUP)
-        return remote(sums_out.at[t, c], sums_in.at[d, c], sum_send.at[c, d], sum_recv.at[c, d], group_peer(d))
+        return remote(sums_out.at[t], sums_in.at[d], sum_send.at[c, d], sum_recv.at[c, d], group_peer(d))
 
     for load in loads[:3]:
         load.wait()
+    pl.semaphore_wait(barrier, 3 + n_pair - 1 + 2)
+    to_right().start()
+    to_left().start()
+    for d in range(1, n_pair):
+        ow_copy(d).start()
     tp_all[pl.ds(pl.multiple_of(r * tok_dev, 16), tok_dev), :] = dot(norm_rows(trunk[...].astype(F32)).astype(BF16), single_w[...]).astype(BF16)
     loads[3].wait()
     w = bias_w[...]
@@ -235,17 +240,10 @@
     def no_outside():
         tp_all[GROUP * tok_dev : (GROUP + 1) * tok_dev, :] = jnp.zeros((tok_dev, LANES), BF16)
 
-    band_chunk(0)
-    pl.semaphore_wait(barrier, 3 + n_pair - 1 + 2)
     for d in (2, 1, 3):
         tp_copy(d).start()
     outside(lambda copy: copy.start())
-    to_right().start()
-    to_left().start()
-    send_bias(0)
-    for d in range(1, n_pair):
-        ow_copy(d).start()
-    for c in range(1, CHUNKS):
+    for c in range(CHUNKS):
         band_chunk(c)
         send_bias(c)
 
@@ -287,7 +285,9 @@
     g_w = jnp.where(head == 2, pltpu.roll(aw32, LANES - 32, 1), 0.0).astype(BF16)
     kv_lane = (head == 1) | (head == 2)
 
-    def key_rows(i, normed):
+    w_all = jnp.concatenate([aw, q_w, g_w], axis=1)
+
+    def key_rows(i, product):
         place = lax.broadcasted_iota(jnp.int32, (LANES, LANES), 0) + (a * atom_dev + (i - 1) * LANES)
         absent = jnp.where((place >= 0) & (place < total_atoms), 0.0, -1e30)
         token = tok_info[i] + LANES
@@ -297,14 +297,15 @@
             jnp.where(lane1 == 1, (token & 15).astype(F32), jnp.where(lane1 == 3, absent, jnp.where((lane1 == 2) | (lane1 == 4), 1.0, 0.0))),
         )
         keys[pl.ds(pl.multiple_of(i * LANES, LANES), LANES), :] = jnp.where(
-            kv_lane, dot(normed, aw).astype(BF16).astype(F32), info
+            kv_lane, product.astype(BF16).astype(F32), info
         )
 
     def proj_block(b, carry):
         rows = pl.ds(pl.multiple_of(b * LANES, LANES), LANES)
         normed = norm_rows(cond[pl.ds(pl.multiple_of(first + b * LANES, LANES), LANES), :].astype(F32)).astype(BF16)
-        key_rows(b + 1, normed)
-        query = jnp.where(lane1 == 3, 1.0, dot(normed, q_w)).astype(BF16)
+        product = dot(normed, w_all)
+        key_rows(b + 1, product[:, :LANES])
+        query = jnp.where(lane1 == 3, 1.0, product[:, LANES : 2 * LANES]).astype(BF16)
         token = tok_info[b + 1] + LANES
         against = jnp.where(
             lane1 == 0,
@@ -322,12 +323,12 @@
         for j in range(4):
             queries[4 * b + j, 0:32, :] = query[32 * j : 32 * j + 32]
             queries[4 * b + j, 32:64, :] = against[32 * j : 32 * j + 32]
-        gate[rows, :] = jax.nn.sigmoid(dot(normed, g_w).astype(BF16).astype(F32))
+        gate[rows, :] = jax.nn.sigmoid(product[:, 2 * LANES :].astype(BF16).astype(F32))
         return carry
 
     lax.fori_loop(0, blocks, proj_block, 0, unroll=True)
     for i in (0, blocks + 1):
-        key_rows(i, norm_rows(cond[i * LANES : (i + 1) * LANES, :].astype(F32)).astype(BF16))
+        key_rows(i, dot(norm_rows(cond[i * LANES : (i + 1) * LANES, :].astype(F32)).astype(BF16), aw))
 
     for d in range(1, n_pair):
         ow_arrive(d).wait_recv()
@@ -397,6 +398,16 @@
     for b in range(blocks // SEND):
         for d in (2, 1, 3):
             gate_copy(b, d).start()
+
+    for d in range(1, GROUP):
+        tp_copy(d).wait_send()
+        for c in range(CHUNKS):
+            sends(d, lambda: bias_copy(c, d).wait_send())
+    outside(lambda copy: copy.wait_send())
+    to_right().wait_send()
+    to_left().wait_send()
+    for d in range(1, n_pair):
+        ow_copy(d).wait_send()
 
     column_blocks = sums.shape[1]
     for k, (begin, end) in enumerate(PARTS):
@@ -426,35 +437,26 @@
                 sums[t, c] = here
                 if k == len(PARTS) - 1:
                     sums_out[t, c] = here.astype(BF16)
-            if k == len(PARTS) - 1:
-                for d in (2, 1, 3):
-                    sends(d, lambda: sum_copy(c, d).start())
+    for d in (2, 1, 3):
+        sends(d, lambda: sum_copy(0, d).start())
+    for d in range(1, n_pair):
+        for b in range(blocks // SEND):
+            gate_copy(b, d).wait_send()
     eye = lax.broadcasted_iota(jnp.int32, (tok_dev, tok_dev), 0) == lax.broadcasted_iota(
         jnp.int32, (tok_dev, tok_dev), 1
     )
     count = jnp.sum(jnp.where(eye, counts[...].astype(F32), 0.0), axis=1, keepdims=True)
     inverse = 1.0 / count
+    for d in range(1, GROUP):
+        receives(d, lambda: sum_copy(0, d).wait_recv())
     for c in range(column_blocks):
-        for d in range(1, GROUP):
-            receives(d, lambda: sum_copy(c, d).wait_recv())
         result = sums[r, c]
         for d in range(1, GROUP):
             result = result + sums_in[d, c].astype(F32)
         token_out[:, c * LANES : (c + 1) * LANES] = (result * inverse).astype(BF16)
 
     for d in range(1, GROUP):
-        tp_copy(d).wait_send()
-        for c in range(column_blocks):
-            sends(d, lambda: sum_copy(c, d).wait_send())
-        for c in range(CHUNKS):
-            sends(d, lambda: bias_copy(c, d).wait_send())
-    for d in range(1, n_pair):
-        ow_copy(d).wait_send()
-        for b in range(blocks // SEND):
-            gate_copy(b, d).wait_send()
-    outside(lambda copy: copy.wait_send())
-    to_right().wait_send()
-    to_left().wait_send()
+        sends(d, lambda: sum_copy(0, d).wait_send())
 
 
 def shards(

time: 30.4 us -> 32.1 us (1.056)
  Pallas kernels: 28.4 us -> 30.1 us
    pallas_call x1, Pallas kernels: 28.4 us -> 30.1 us  [shards(): pl.pallas_call(functools.partial(kernel, (n_dev, n_pair, total_atoms)), o...]
where the time goes in v4:
time: 32.1 us
  Pallas kernels  30.1 us (94%)
  local copies, waits for them, and re-layouts  1.31 us (4%)
  between operations  0.64 us (2%)
    pallas_call x1, Pallas kernels, shards(): pl.pallas_call(functools.partial(kernel, (n_dev, n_pair, total_atoms)), o...  30.1 us
    unnamed x2, local copies, waits for them, and re-layouts  1.31 us

profile of v4, /device:TPU:1, one launch (start us, length us, event | category | flops | bytes accessed | tf_op | source)
XLA Modules:
  0.0 32.1 jit_solution(7707014858032818266)
XLA Ops:
  0.6 30.1 %encoder.1 = (bf16[768,128]{1,0:T(8,128)(2,1)S(1)}, bf16[96,384]{1,0:T(8,128)(2,1)S(1)}) custom-call(bf16[96,384]{1,0:T(8,128)(2,1)} %trunk_h.1, bf16[768,128]{1,0:T(8,128)(2,1)} %feat_h.1, bf16[96,256,128]{2,1,0:T(8,128)(2,1)} %band.1, s32[384,128]{1,0:T(8,128)} %bitcast.4, s32[1,96]{1,0:T(1,128)} %bitcast.6, s32[24]{0:T(128)} %koff_h.1, ...), custom_call_target="tpu_custom_call" | custom-call | tf_op jit(solution)/shard_map/encoder/pallas_call | solution.py:476
  30.8 0.7 %copy.15 = bf16[768,128]{1,0:T(8,128)(2,1)} copy(bf16[768,128]{1,0:T(8,128)(2,1)S(1)} %get-tuple-element.4) | data formatting | bytes 393216
  31.4 0.6 %copy.16 = bf16[96,384]{1,0:T(8,128)(2,1)} copy(bf16[96,384]{1,0:T(8,128)(2,1)S(1)} %get-tuple-element.5) | data formatting | bytes 147456
